TPU v7x, 512 devices: a whole 4x4x16 slice. The times are simulated.
512 devices in a mesh: dp: 32 (over x, y, core), expert: 16 (over z).
Axes of the slice: x: 4, y: 4, z: 16, core: 2. Of those that a mesh axis runs over, the one named last changes fastest.
Arguments:
- grad_out: bfloat16 [2048, 6144], P('expert', 'dp'), may hold values from -48 to 48
- routes: int32 [2048, 4], P('expert'), may hold values from 0 to 15, all different within a row; in each aligned block of 128 rows (0 to 127, 128 to 255, ...) at most 40 rows name the same one
- probs: float32 [2048, 4], P('expert'), may hold values from 0.05 to 0.6
- resp_len: int32 [16, 4], P('expert'), may hold values from 1 to 64, 128 in all within a row
- w_down: bfloat16 [16, 5376, 6144], P('expert', 'dp'), may hold values from -0.078125 to 0.078125
- w_up: bfloat16 [16, 6144, 5376], P('expert', 'dp'), may hold values from -0.078125 to 0.078125
- gate_act: bfloat16 [16, 640, 5376], P('expert', None, 'dp'), may hold values from -6 to 6
Outputs:
- grad_in: bfloat16 [2048, 6144], P('expert', 'dp')
Inputs may be any that keep to these rules, and one draw needn't show every extreme that they name: `routes`: within each aligned block of 128 rows (one shard) no expert is named more than 40 times, a bound that some block reaches. `resp_len`: each row sums to 128, and its largest entry is 64.
All inputs are finite; a program needn't handle non-finite values.
Results may differ from a plain program's by a relative error of at most 0.013.
Values may be sent and summed in bfloat16 or wider, within the bound.
No kernel may reach another device: no remote copies, remote signals or barrier semaphores. Data moves between devices by JAX's collectives and lax.ppermute only.
A program may use at most 64 MiB of HBM per device.

v0:
```python
import jax
import jax.numpy as jnp
from jax import lax
from jax.sharding import PartitionSpec as P


def token_weight(resp_len, rows):
    lengths = resp_len[0]
    ends = jnp.cumsum(lengths)
    starts = ends - lengths
    position = jnp.arange(rows, dtype=jnp.int32)[:, None]
    inside = (position >= starts[None, :]) & (position < ends[None, :])
    inverse = 1.0 / lengths.astype(jnp.float32)
    return jnp.sum(jnp.where(inside, inverse[None, :], jnp.zeros_like(inverse)[None, :]), axis=1)


def slot_index(routes, experts, capacity):
    labels = jnp.arange(experts, dtype=jnp.int32)
    hits = (routes[:, :, None] == labels[None, None, :]).astype(jnp.int32)
    per_row = jnp.sum(hits, axis=1)
    before = jnp.cumsum(per_row, axis=0) - per_row
    position = jnp.sum(hits * before[:, None, :], axis=2)
    return routes * capacity + position


def contract(left, right):
    return lax.dot_general(
        left, right, (((1,), (1,)), ((), ())), preferred_element_type=jnp.float32
    )


def on_device(grad_out, routes, probs, resp_len, w_down, w_up, gate_act):
    tokens_here, width_here = grad_out.shape
    picks = routes.shape[1]
    experts = lax.axis_size("expert")
    capacity = min(
        tokens_here, tokens_here * picks // experts + tokens_here * picks // (4 * experts)
    )
    slots = experts * capacity
    weight = token_weight(resp_len, tokens_here)
    target = slot_index(routes, experts, capacity).reshape(-1)
    factor = probs * weight[:, None]
    scaled = (grad_out[:, None, :].astype(jnp.float32) * factor[:, :, None]).astype(jnp.bfloat16)
    selector = (jnp.arange(slots, dtype=jnp.int32)[:, None] == target[None, :]).astype(jnp.bfloat16)
    outgoing = jnp.dot(
        selector,
        scaled.reshape(tokens_here * picks, width_here),
        preferred_element_type=jnp.float32,
    ).astype(jnp.bfloat16)
    arrived = lax.all_to_all(
        outgoing.reshape(experts, capacity, width_here),
        "expert",
        split_axis=0,
        concat_axis=0,
        tiled=True,
    ).reshape(slots, width_here)
    down_rows = w_down[0]
    up_rows = w_up[0]
    saved = gate_act[0]
    full_rows = lax.all_gather(arrived, "dp", axis=1, tiled=True)
    hidden_sum = contract(full_rows, down_rows)
    hidden_grad = (hidden_sum * saved.astype(jnp.float32)).astype(jnp.bfloat16)
    full_hidden = lax.all_gather(hidden_grad, "dp", axis=1, tiled=True)
    product = contract(full_hidden, up_rows)
    returning = product.astype(jnp.bfloat16)
    back = lax.all_to_all(
        returning.reshape(experts, capacity, width_here),
        "expert",
        split_axis=0,
        concat_axis=0,
        tiled=True,
    ).reshape(slots, width_here)
    picked = (
        jnp.take(back, target, axis=0).reshape(tokens_here, picks, width_here).astype(jnp.float32)
    )
    return jnp.sum(picked, axis=1).astype(jnp.bfloat16)


def solution(mesh):
    in_specs = (
        P("expert", "dp"),
        P("expert", None),
        P("expert", None),
        P("expert", None),
        P("expert", "dp", None),
        P("expert", "dp", None),
        P("expert", None, "dp"),
    )
    out_specs = P("expert", "dp")
    return jax.shard_map(
        on_device, mesh=mesh, in_specs=in_specs, out_specs=out_specs, check_vma=False
    )
```

profile of v0, /device:TPU:2, one launch (start us, length us, event | category | flops | bytes accessed | tf_op | source)
XLA Modules:
  0.0 234.0 jit_solution(2945897742113075317)
XLA Ops:
  6.5 0.0 copy-start
  6.5 0.0 all-gather.3.cloned.1.call-start
  6.5 0.8 divide_bitcast_fusion
  7.3 0.8 reduce-window.4
  8.2 0.7 fusion.18
  8.8 0.7 convert_reduce_fusion
  9.5 0.1 copy.30
  9.6 0.1 select_reduce_fusion.2
  9.7 0.7 broadcast_multiply_fusion
  10.4 0.1 copy.36
  10.5 0.1 mul.51
  10.6 0.2 reduce_window_sum.18
  10.8 0.1 copy.32
  10.9 0.7 select_reduce_fusion.1
  11.6 0.7 compare_and_fusion
  12.3 0.1 copy.34
  12.4 0.1 reshape.88
  12.5 0.9 copy.35
  13.4 0.1 mul.47
  13.5 0.2 mul.48
  13.7 0.5 fusion.8
  14.2 0.2 copy.37
  14.4 35.8 %all_to_all.10 = bf16[16,40,192]{2,1,0:T(8,128)(2,1)S(1)} all-to-all(bf16[16,40,192]{2,1,0:T(8,128)(2,1)S(1)} %bitcast.33), channel_id=1, replica_groups=mesh['dp'=32,'expert'=16] {'expert'}, dimensions={0} | all-to-all | bytes 491520 | tf_op jit(solution)/shard_map/all_to_all | solution.py:50
  50.2 0.9 copy.38
  51.0 0.0 all-gather.3.cloned.1.call-update
  51.0 0.0 all-gather.5.cloned.1.call-start
  51.1 62.5 %all-gather.3.cloned.1.call-done = bf16[640,6144]{0,1:T(8,128)(2,1)} async-done(((bf16[640,192]{0,1:T(8,128)(2,1)}), bf16[640,6144]{0,1:T(8,128)(2,1)}) %all-gather.3.cloned.1.call-update) | async-done | bytes 7864336 | tf_op jit(solution)/shard_map/all_gather | solution.py:60
  113.6 6.3 %fusion.12 = bf16[640,168]{0,1:T(8,128)(2,1)} fusion(bf16[640,6144]{0,1:T(8,128)(2,1)} %all-gather.3.cloned.1.call-done, bf16[1,168,6144]{2,1,0:T(8,128)(2,1)} %param.11, bf16[1,640,168]{1,2,0:T(8,128)(2,1)} %param.13), kind=kOutput, calls=%fused_computation.10 | convolution fusion | flops 1321528320 | bytes 10358784 | tf_op jit(solution)/shard_map/dot_general | solution.py:27
  120.0 0.0 all-gather.5.cloned.1.call-update
  120.0 64.6 %all-gather.5.cloned.1.call-done = bf16[640,5376]{0,1:T(8,128)(2,1)} async-done(((bf16[640,168]{0,1:T(8,128)(2,1)}), bf16[640,5376]{0,1:T(8,128)(2,1)}) %all-gather.5.cloned.1.call-update) | async-done | bytes 6881296 | tf_op jit(solution)/shard_map/all_gather | solution.py:63
  184.6 0.0 copy-done
  184.6 4.7 %fusion.9 = bf16[640,192]{0,1:T(8,128)(2,1)S(1)} fusion(bf16[640,5376]{0,1:T(8,128)(2,1)} %all-gather.5.cloned.1.call-done, bf16[1,192,5376]{2,1,0:T(8,128)(2,1)S(1)} %copy-done), kind=kOutput, calls=%fused_computation.9 | convolution fusion | flops 1321328640 | bytes 9191424 | tf_op jit(solution)/shard_map/dot_general | solution.py:27
  189.3 0.9 copy.39
  190.2 12.3 %all-to-all-start.1 = ((bf16[16,40,192]{2,1,0:T(8,128)(2,1)}), bf16[16,40,192]{2,1,0:T(8,128)(2,1)S(1)}, u32[]{:S(2)}, u32[]{:S(2)}) async-start(bf16[16,40,192]{2,1,0:T(8,128)(2,1)} %bitcast.10), calls=%async_computation.1 | async-start | bytes 655360 | tf_op jit(solution)/shard_map/all_to_all | solution.py:66
  202.5 0.1 reshape.95
  202.6 0.1 copy.33
  202.8 21.2 %all-to-all-done.1 = bf16[16,40,192]{2,1,0:T(8,128)(2,1)S(1)} async-done(((bf16[16,40,192]{2,1,0:T(8,128)(2,1)}), bf16[16,40,192]{2,1,0:T(8,128)(2,1)S(1)}, u32[]{:S(2)}, u32[]{:S(2)}) %all-to-all-start.1) | async-done | bytes 245792 | tf_op jit(solution)/shard_map/all_to_all | solution.py:66
  224.0 1.9 gather_fusion
  226.0 0.1 gather.7
  226.1 0.4 select_reduce_fusion
  226.4 0.7 copy.41
  (3 shorter events, 0.0 us)
Async XLA Ops:
  6.5 178.1 %copy-start = (bf16[1,192,5376]{2,1,0:T(8,128)(2,1)S(1)}, bf16[1,192,5376]{2,1,0:T(8,128)(2,1)}, u32[]{:S(2)}) copy-start(bf16[1,192,5376]{2,1,0:T(8,128)(2,1)} %param.12) | copy-start | bytes 6193156
  6.5 107.1 %all-gather.3.cloned.1.call-start = ((), (), s32[]{:S(2)}) async-start(), calls=%async_computation.2 | async-start | bytes 8110080 | tf_op jit(solution)/shard_map/all_gather | solution.py:60
  51.0 133.6 %all-gather.5.cloned.1.call-start = ((), (), s32[]{:S(2)}) async-start(), calls=%async_computation.3 | async-start | bytes 7096320 | tf_op jit(solution)/shard_map/all_gather | solution.py:63
  190.2 33.8 %all-to-all-start.1 = ((bf16[16,40,192]{2,1,0:T(8,128)(2,1)}), bf16[16,40,192]{2,1,0:T(8,128)(2,1)S(1)}, u32[]{:S(2)}, u32[]{:S(2)}) async-start(bf16[16,40,192]{2,1,0:T(8,128)(2,1)} %bitcast.10), calls=%async_computation.1 | async-start | bytes 655360 | tf_op jit(solution)/shard_map/all_to_all | solution.py:66
Sparse Core Ops, SparseCore 0:
  51.2 62.4 all-gather.2
  120.1 64.4 all-gather.4
where the time goes:
time: 234 us
  waiting for transfers between devices  148 us (63%)
  blocking collectives  35.8 us (15%)
  between operations  13.5 us (6%)
  starting transfers between devices  12.3 us (5%)
  matrix products  11.5 us (5%)
  local copies, waits for them, and re-layouts  6.7 us (3%)
  other arithmetic  5.74 us (2%)
    all_gather x1, waiting for transfers between devices, on_device(): full_hidden = lax.all_gather(hidden_grad, 'dp', axis=1, tiled=True)  64.6 us
    all_gather x1, waiting for transfers between devices, on_device(): full_rows = lax.all_gather(arrived, 'dp', axis=1, tiled=True)  62.5 us
    all_to_all x1, blocking collectives, on_device(): lax.all_to_all(outgoing.reshape(experts, capacity, width_here), 'expert',...  35.8 us
    all_to_all x1, waiting for transfers between devices, on_device(): lax.all_to_all(returning.reshape(experts, capacity, width_here), 'expert'...  21.2 us
    all_to_all x1, starting transfers between devices, on_device(): lax.all_to_all(returning.reshape(experts, capacity, width_here), 'expert'...  12.3 us
    dot_general x2, matrix products, contract(): lax.dot_general(left, right, (((1,), (1,)), ((), ())), preferred_element_...  11 us
  transfers between devices with their start and end apart: 3, of which 3 were waited for; matrix products, arithmetic and copies ran while one was open for 0% of the time, Pallas kernels for 0%

commit v1 on v0

v1 whole, which is shorter than its diff:
```python
import functools

import jax
import jax.numpy as jnp
from jax import lax
from jax.experimental import pallas as pl
from jax.experimental.pallas import tpu as pltpu
from jax.sharding import PartitionSpec as P

SIDE = 4
CORES = 2
EXPERTS = 16
CAPACITY = 40
SLOTS = EXPERTS * CAPACITY
LANES = 128
PIECES = LANES // CAPACITY
MIB = 1 << 20
MOST = 58 * MIB


def index(x, y, c):
    return ((x % SIDE) * SIDE + y % SIDE) * CORES + c


X_GROUPS = [[index(x, y, c) for x in range(SIDE)] for y in range(SIDE) for c in range(CORES)]
Y_GROUPS = [[index(x, y, c) for y in range(SIDE)] for x in range(SIDE) for c in range(CORES)]


def moves(dx, dy, swap=0):
    return [
        (index(x, y, c), index(x + dx, y + dy, (c + swap) % CORES))
        for x in range(SIDE)
        for y in range(SIDE)
        for c in range(CORES)
    ]


OTHER_CORE = moves(0, 0, 1)


def exchange(blocks, groups):
    return lax.all_to_all(blocks, "dp", 0, 0, tiled=True, axis_index_groups=groups)


def after(value, *others):
    return lax.optimization_barrier((value, *others))[0]


def call(kernel, out_shape, n_scalars, n_arrays, limit=6 * MIB, scratch=(), flops=0, moved=0):
    return pl.pallas_call(
        kernel,
        out_shape=out_shape,
        in_specs=[pl.BlockSpec(memory_space=pltpu.SMEM)] * n_scalars
        + [pl.BlockSpec(memory_space=pltpu.VMEM)] * n_arrays,
        out_specs=jax.tree.map(lambda _: pl.BlockSpec(memory_space=pltpu.VMEM), out_shape),
        scratch_shapes=scratch,
        compiler_params=pltpu.CompilerParams(vmem_limit_bytes=limit),
        cost_estimate=pl.CostEstimate(flops=flops, bytes_accessed=moved, transcendentals=0),
    )


def iota(shape, dim):
    return lax.broadcasted_iota(jnp.int32, shape, dim)


def pieces(shape, dim=1):
    at = iota(shape, dim)
    piece = jnp.zeros(shape, jnp.int32)
    for i in range(1, PIECES + 1):
        piece = piece + jnp.where(at >= i * CAPACITY, 1, 0)
    return piece, at - piece * CAPACITY


def held_slots(tokens):
    piece, within = pieces((LANES, tokens), 0)
    return jnp.where(piece < PIECES, within, -2).astype(jnp.float32)


def dispatch_kernel(lengths, routes_ref, probs_ref, grad_ref, out_ref, slot_ref):
    width, tokens = grad_ref.shape
    at = iota((1, tokens), 1)
    weight = jnp.zeros((1, tokens), jnp.float32)
    start = jnp.int32(0)
    for i in range(lengths.shape[1]):
        length = lengths[0, i]
        inverse = 1.0 / jnp.full((1, tokens), length, jnp.int32).astype(jnp.float32)
        weight = weight + jnp.where((at >= start) & (at < start + length), inverse, 0.0)
        start = start + length

    label = iota((EXPERTS, tokens), 0)
    hits = jnp.zeros((EXPERTS, tokens), jnp.float32)
    factor = jnp.zeros((EXPERTS, tokens), jnp.float32)
    for k in range(routes_ref.shape[0]):
        named = routes_ref[k : k + 1, :] == label
        hits = hits + jnp.where(named, 1.0, 0.0)
        factor = factor + jnp.where(named, probs_ref[k : k + 1, :] * weight, 0.0)
    above = (iota((tokens, tokens), 0) < iota((tokens, tokens), 1)).astype(jnp.bfloat16)
    before = jnp.dot(hits.astype(jnp.bfloat16), above, preferred_element_type=jnp.float32)
    slot = jnp.where(hits > 0.0, before, -1.0)
    slot_ref[...] = slot

    piece, _ = pieces((1, LANES))
    held = held_slots(tokens)
    chunk = width // PIECES
    source = grad_ref[...].astype(jnp.float32)
    for e in range(EXPERTS):
        pick = jnp.where(slot[e : e + 1, :] == held, 1.0, 0.0).astype(jnp.bfloat16)
        scaled = (source * factor[e : e + 1, :]).astype(jnp.bfloat16)
        full = lax.dot_general(scaled, pick, (((1,), (1,)), ((), ())), preferred_element_type=jnp.float32)
        chosen = full[0:chunk]
        for q in range(1, PIECES):
            chosen = jnp.where(piece == q, full[q * chunk : (q + 1) * chunk], chosen)
        out_ref[e] = chosen.astype(jnp.bfloat16)


def unpack_kernel(in_ref, out_ref):
    shards, chunk, _ = in_ref.shape
    blocks = [in_ref[s].astype(jnp.float32) for s in range(shards)]
    lane = iota((1, LANES), 1)
    for q in range(PIECES):
        turned = [
            pltpu.roll(blocks[s], ((s - q) * CAPACITY) % LANES, 1) if ((s - q) * CAPACITY) % LANES else blocks[s]
            for s in range(shards)
        ]
        for b in range(SLOTS // LANES):
            block = jnp.zeros((chunk, LANES), jnp.float32)
            for s in range(shards):
                low = max(s * CAPACITY - b * LANES, 0)
                high = min((s + 1) * CAPACITY - b * LANES, LANES)
                if low < high:
                    block = jnp.where((lane >= low) & (lane < high), turned[s], block)
            block = block.astype(jnp.bfloat16)
            for n in range(out_ref.shape[0]):
                out_ref[n, q * chunk : (q + 1) * chunk, b * LANES : (b + 1) * LANES] = block


def product_kernel(along, copied, place, own_ref, other_ref, *refs):
    weights, out_ref, data = refs[:SIDE], refs[SIDE], refs[SIDE + 1]
    copies = []
    if copied:
        held, sems = refs[SIDE + 2 : -1], refs[-1]
        copies = [pltpu.make_async_copy(weights[k], held[k], sems.at[k]) for k in range(SIDE)]
        weights = held
    for copy in copies:
        copy.start()
    deep = own_ref.shape[1]
    for core in range(CORES):

        @pl.when(place[2] == core)
        def _(core=core):
            both = (own_ref, other_ref) if core == 0 else (other_ref, own_ref)
            for n in range(SIDE):
                data[2 * n * deep : 2 * (n + 1) * deep, :] = jnp.concatenate([ref[n] for ref in both], axis=0)

    for k in range(SIDE):
        if copied:
            copies[k].wait()
        part = jnp.dot(weights[k][...], data[...], preferred_element_type=jnp.float32)
        out_ref[lax.rem(place[along] + SIDE - k, SIDE)] = part.astype(jnp.bfloat16)


def added(in_ref):
    total = in_ref[0].astype(jnp.float32)
    for n in range(1, in_ref.shape[0]):
        total = total + in_ref[n].astype(jnp.float32)
    return total


def gate_kernel(in_ref, gate_ref, out_ref):
    hidden = (added(in_ref) * gate_ref[...].astype(jnp.float32)).astype(jnp.bfloat16)
    for n in range(out_ref.shape[0]):
        out_ref[n] = hidden


def pack_kernel(in_ref, out_ref):
    shards, chunk, _ = out_ref.shape
    total = added(in_ref)
    piece, _ = pieces((1, LANES))
    lane = iota((1, LANES), 1)
    for s in range(shards):
        b, low = divmod(s * CAPACITY, LANES)
        block = jnp.zeros((chunk, LANES), jnp.float32)
        for q in range(PIECES):
            rows = total[q * chunk : (q + 1) * chunk]
            part = rows[:, b * LANES : (b + 1) * LANES]
            if low + CAPACITY > LANES:
                part = jnp.where(lane >= low, part, rows[:, (b + 1) * LANES : (b + 2) * LANES])
            turn = (q * CAPACITY - low) % LANES
            block = jnp.where(piece == q, pltpu.roll(part, turn, 1) if turn else part, block)
        out_ref[s] = block.astype(jnp.bfloat16)


def combine_kernel(in_ref, slot_ref, out_ref):
    piece, _ = pieces((1, LANES))
    held = held_slots(slot_ref.shape[1])
    total = jnp.zeros(out_ref.shape, jnp.float32)
    for e in range(in_ref.shape[0]):
        block = in_ref[e].astype(jnp.float32)
        spread = jnp.concatenate([jnp.where(piece == q, block, 0.0) for q in range(PIECES)], axis=0)
        pick = jnp.where(slot_ref[e : e + 1, :] == held, 1.0, 0.0).astype(jnp.bfloat16)
        total = total + jnp.dot(spread.astype(jnp.bfloat16), pick, preferred_element_type=jnp.float32)
    out_ref[...] = total.astype(jnp.bfloat16)


def cut_down_kernel(place, in_ref, *refs):
    out_refs, held, into, out_of = refs[:SIDE], refs[SIDE : 2 * SIDE], refs[-2], refs[-1]
    wide = in_ref.shape[1] // (SIDE * SIDE)

    def taken(k, n):
        block = n * SIDE + lax.rem(place[1] + k, SIDE)
        return pltpu.make_async_copy(
            in_ref.at[:, pl.ds(pl.multiple_of(block * wide, wide), wide)],
            held[k].at[:, pl.ds(n * wide, wide)],
            into.at[k, n],
        )

    def given(k):
        return pltpu.make_async_copy(held[k], out_refs[k], out_of.at[k])

    order = (1, 3, 2, 0)
    for k in order:
        for n in range(SIDE):
            taken(k, n).start()
    for k in order:
        for n in range(SIDE):
            taken(k, n).wait()
        given(k).start()
    for k in order:
        given(k).wait()


def cut_up_kernel(place, in_ref, *refs):
    out_refs, whole, held, into, out_of = refs[:SIDE], refs[SIDE], refs[SIDE + 1 : -2], refs[-2], refs[-1]
    fetch = pltpu.make_async_copy(in_ref, whole, into)
    fetch.start()
    fetch.wait()
    wide = in_ref.shape[1] // SIDE
    for at in range(SIDE):

        @pl.when(place[0] == at)
        def _(at=at):
            for k in range(SIDE):
                n = (at + k) % SIDE
                held[k][...] = whole[:, n * wide : (n + 1) * wide]

    copies = [pltpu.make_async_copy(held[k], out_refs[k], out_of.at[k]) for k in range(SIDE)]
    for copy in copies:
        copy.start()
    for copy in copies:
        copy.wait()


def cut(kernel, place, weights, whole, sems):
    part = jax.ShapeDtypeStruct((weights.shape[0], weights.shape[1] // SIDE), weights.dtype)
    in_hbm = pl.BlockSpec(memory_space=pltpu.HBM)
    return list(
        pl.pallas_call(
            kernel,
            out_shape=[part] * SIDE,
            in_specs=[pl.BlockSpec(memory_space=pltpu.SMEM), in_hbm],
            out_specs=[in_hbm] * SIDE,
            scratch_shapes=[pltpu.VMEM(weights.shape, weights.dtype)] * whole
            + [pltpu.VMEM(part.shape, part.dtype)] * SIDE
            + [pltpu.SemaphoreType.DMA(shape) for shape in sems],
            compiler_params=pltpu.CompilerParams(vmem_limit_bytes=MOST),
        )(place, weights)
    )


def send(part, dx, dy):
    return lax.ppermute(part, "dp", moves(dx, dy))


def product(along, copied, place, rows, weights):
    other = lax.ppermute(rows, "dp", OTHER_CORE)
    _, deep, slots = rows.shape
    in_vmem = pl.BlockSpec(memory_space=pltpu.VMEM)
    scratch = [pltpu.VMEM((CORES * SIDE * deep, slots), jnp.bfloat16)]
    if copied:
        scratch += [pltpu.VMEM(part.shape, part.dtype) for part in weights]
        scratch += [pltpu.SemaphoreType.DMA((SIDE,))]
    return pl.pallas_call(
        functools.partial(product_kernel, along, copied),
        out_shape=jax.ShapeDtypeStruct((SIDE, weights[0].shape[0], slots), jnp.bfloat16),
        in_specs=[pl.BlockSpec(memory_space=pltpu.SMEM)]
        + [in_vmem] * 2
        + [pl.BlockSpec(memory_space=pltpu.HBM) if copied else in_vmem] * SIDE,
        out_specs=in_vmem,
        scratch_shapes=scratch,
        compiler_params=pltpu.CompilerParams(vmem_limit_bytes=MOST if copied else 12 * MIB),
    )(place, rows, other, *weights)


def on_device(grad_out, routes, probs, resp_len, w_down, w_up, gate_act):
    tokens, width = grad_out.shape
    hidden = w_down.shape[1]
    chunk = width // PIECES
    me = lax.axis_index("dp")
    place = jnp.stack([me // (SIDE * CORES), (me // CORES) % SIDE, me % CORES]).astype(jnp.int32)

    def half(*shape):
        return jax.ShapeDtypeStruct(shape, jnp.bfloat16)

    outgoing, slots = call(
        dispatch_kernel, (half(EXPERTS, chunk, LANES), jax.ShapeDtypeStruct((EXPERTS, tokens), jnp.float32)), 1, 3
    )(resp_len, routes.T, probs.T, grad_out.T)
    together = lax.optimization_barrier

    down = cut(cut_down_kernel, place, w_down[0], 0, [(SIDE, SIDE), (SIDE,)])
    outgoing, down = together((outgoing, down))
    arrived = lax.all_to_all(outgoing, "expert", 0, 0, tiled=True)
    arrived, down[1], down[3] = together((arrived, send(down[1], 0, 1), send(down[3], 0, 3)))

    spread = call(unpack_kernel, half(SIDE, width, SLOTS), 0, 1)(arrived)
    spread, down[2], up = together((spread, down[2], w_up[0]))
    rows = exchange(spread, X_GROUPS)
    up = cut(cut_up_kernel, place, up, 1, [(), (SIDE,)])
    rows, down[2], up = together((rows, send(down[2], 0, 2), up))

    partial = product(1, True, place, rows, down)
    partial, up = together((partial, up))
    sums = exchange(partial, Y_GROUPS)
    sums, up[1], up[3] = together((sums, send(up[1], 1, 0), send(up[3], 3, 0)))
    spread = call(gate_kernel, half(SIDE, hidden, SLOTS), 0, 2)(sums, gate_act[0].T)
    spread, up[2] = together((spread, up[2]))
    rows = exchange(spread, Y_GROUPS)
    rows, up[2] = together((rows, send(up[2], 2, 0)))
    partial = product(0, False, place, rows, up)
    returning = call(pack_kernel, half(EXPERTS, chunk, LANES), 0, 1)(exchange(partial, X_GROUPS))
    back = lax.all_to_all(returning, "expert", 0, 0, tiled=True)
    return call(combine_kernel, half(width, tokens), 0, 2)(back, slots).T


def solution(mesh):
    in_specs = (
        P("expert", "dp"),
        P("expert", None),
        P("expert", None),
        P("expert", None),
        P("expert", "dp", None),
        P("expert", "dp", None),
        P("expert", None, "dp"),
    )
    out_specs = P("expert", "dp")
    return jax.shard_map(
        on_device, mesh=mesh, in_specs=in_specs, out_specs=out_specs, check_vma=False
    )
```

time: 234 us -> 174 us (0.74)
  the two profiles are of different devices: /device:TPU:2 before, /device:TPU:8 now
where the time goes in v1:
time: 174 us; the launch traced here: 173 us
  starting transfers between devices  54.7 us (31%)
  blocking collectives  47.5 us (27%)
  waiting for transfers between devices  47.4 us (27%)
  Pallas kernels  21.5 us (12%)
    ppermute x6, waiting for transfers between devices, send(): return lax.ppermute(part, 'dp', moves(dx, dy))  42.5 us
    all_to_all x1, blocking collectives, on_device(): back = lax.all_to_all(returning, 'expert', 0, 0, tiled=True)  29 us
    ppermute x6, starting transfers between devices, send(): return lax.ppermute(part, 'dp', moves(dx, dy))  21.7 us
    all_to_all x1, blocking collectives, exchange(): lax.all_to_all(blocks, 'dp', 0, 0, tiled=True, axis_index_groups=groups)  18.5 us
    all_to_all x1, starting transfers between devices, on_device(): arrived = lax.all_to_all(outgoing, 'expert', 0, 0, tiled=True)  15.2 us
    all_to_all x3, starting transfers between devices, exchange(): lax.all_to_all(blocks, 'dp', 0, 0, tiled=True, axis_index_groups=groups)  13.8 us
    pallas_call x2, Pallas kernels, product(): pl.pallas_call(functools.partial(product_kernel, along, copied), out_shap...  8.58 us
    pallas_call x2, Pallas kernels, cut(): pl.pallas_call(kernel, out_shape=[part] * SIDE, in_specs=[pl.BlockSpec(me...  7.42 us
  transfers between devices with their start and end apart: 12, of which 8 were waited for; matrix products, arithmetic and copies ran while one was open for 0% of the time, Pallas kernels for 2%

profile of v1, /device:TPU:8, one launch (start us, length us, event | category | flops | bytes accessed | tf_op | source)
XLA Modules:
  0.0 172.9 jit_solution(13785691245795097563)
XLA Ops:
  0.0 0.0 copy-start.2
  0.1 0.6 pad_add_fusion.place
  0.7 3.3 %shard_map.74 = (bf16[168,1536]{1,0:T(8,128)(2,1)}, bf16[168,1536]{1,0:T(8,128)(2,1)}, bf16[168,1536]{1,0:T(8,128)(2,1)}, bf16[168,1536]{1,0:T(8,128)(2,1)}) custom-call(s32[3]{0:T(128)} %pad_add_fusion.place, bf16[168,6144]{1,0:T(8,128)(2,1)} %bitcast.16), custom_call_target="tpu_custom_call" | custom-call | tf_op jit(solution)/shard_map/pallas_call | solution.py:257
  4.0 0.0 copy-start.13
  4.0 0.0 copy-done.6
  4.0 0.0 copy-done.5
  4.1 0.0 copy-done.4
  4.1 0.0 copy-done.2
  4.1 1.9 %shard_map.73 = (bf16[16,64,128]{2,1,0:T(8,128)(2,1)}, f32[16,128]{1,0:T(8,128)S(1)}) custom-call(s32[1,4]{1,0:T(1,128)S(1)} %copy-done.6, s32[4,128]{1,0:T(4,128)S(1)} %bitcast.14, f32[4,128]{1,0:T(4,128)S(1)} %bitcast.15, bf16[192,128]{1,0:T(8,128)(2,1)S(1)} %bitcast.13), custom_call_target="tpu_custom_call" | custom-call | tf_op jit(solution)/shard_map/pallas_call | solution.py:304
  5.9 15.2 %all-to-all-start = ((bf16[16,64,128]{2,1,0:T(8,128)(2,1)}), bf16[16,64,128]{2,1,0:T(8,128)(2,1)S(1)}, u32[]{:S(2)}, u32[]{:S(2)}) async-start(bf16[16,64,128]{2,1,0:T(8,128)(2,1)} %get-tuple-element.49), calls=%async_computation | async-start | bytes 524288 | tf_op jit(solution)/shard_map/all_to_all | solution.py:311
  21.1 3.5 %collective-permute-start = (bf16[168,1536]{1,0:T(8,128)(2,1)}, bf16[168,1536]{1,0:T(8,128)(2,1)S(1)}, u32[]{:S(2)}, u32[]{:S(2)}) collective-permute-start(bf16[168,1536]{1,0:T(8,128)(2,1)} %get-tuple-element.50), channel_id=1, source_target_pairs={{0,32},{16,48},{32,64},{48,80},{64,96},{80,112},{96,0},{112,16},{1... | collective-permute-start | bytes 1548296 | tf_op jit(solution)/shard_map/ppermute | solution.py:271
  24.6 2.4 %collective-permute-start.1 = (bf16[168,1536]{1,0:T(8,128)(2,1)}, bf16[168,1536]{1,0:T(8,128)(2,1)S(1)}, u32[]{:S(2)}, u32[]{:S(2)}) collective-permute-start(bf16[168,1536]{1,0:T(8,128)(2,1)} %get-tuple-element.51), channel_id=1, source_target_pairs={{0,96},{16,112},{32,0},{48,16},{64,32},{80,48},{96,64},{112,80},{1... | collective-permute-start | bytes 1548296 | tf_op jit(solution)/shard_map/ppermute | solution.py:271
  27.0 9.5 %collective-permute-done.refs_1_ = bf16[168,1536]{1,0:T(8,128)(2,1)S(1)} collective-permute-done((bf16[168,1536]{1,0:T(8,128)(2,1)}, bf16[168,1536]{1,0:T(8,128)(2,1)S(1)}, u32[]{:S(2)}, u32[]{:S(2)}) %collective-permute-start) | collective-permute-done | bytes 516128 | tf_op jit(solution)/shard_map/ppermute | solution.py:271
  36.5 3.2 %collective-permute-done.1.refs_3_ = bf16[168,1536]{1,0:T(8,128)(2,1)S(1)} collective-permute-done((bf16[168,1536]{1,0:T(8,128)(2,1)}, bf16[168,1536]{1,0:T(8,128)(2,1)S(1)}, u32[]{:S(2)}, u32[]{:S(2)}) %collective-permute-start.1) | collective-permute-done | bytes 516128 | tf_op jit(solution)/shard_map/ppermute | solution.py:271
  39.7 0.0 all-to-all-done.in_ref
  39.7 1.2 shard_map.75
  40.9 4.3 %all-to-all-start.1 = ((bf16[4,192,640]{2,1,0:T(8,128)(2,1)}), bf16[4,192,640]{2,1,0:T(8,128)(2,1)S(1)}, u32[]{:S(2)}, u32[]{:S(2)}) async-start(bf16[4,192,640]{2,1,0:T(8,128)(2,1)} %shard_map.75), calls=%async_computation.1 | async-start | bytes 1966080 | tf_op jit(solution)/shard_map/all_to_all | solution.py:42
  45.2 4.1 %collective-permute-start.2 = (bf16[168,1536]{1,0:T(8,128)(2,1)S(1)}, bf16[168,1536]{1,0:T(8,128)(2,1)S(1)}, u32[]{:S(2)}, u32[]{:S(2)}) collective-permute-start(bf16[168,1536]{1,0:T(8,128)(2,1)S(1)} %copy-done.13), channel_id=1, source_target_pairs={{0,64},{16,80},{32,96},{48,112},{64,0},{80,16},{96,32},{112,48},{1... | collective-permute-start | bytes 1548296 | tf_op jit(solution)/shard_map/ppermute | solution.py:271
  49.3 4.1 %shard_map.76 = (bf16[192,1344]{1,0:T(8,128)(2,1)}, bf16[192,1344]{1,0:T(8,128)(2,1)}, bf16[192,1344]{1,0:T(8,128)(2,1)}, bf16[192,1344]{1,0:T(8,128)(2,1)}) custom-call(s32[3]{0:T(128)} %pad_add_fusion.place, bf16[192,5376]{1,0:T(8,128)(2,1)} %bitcast.17), custom_call_target="tpu_custom_call" | custom-call | tf_op jit(solution)/shard_map/pallas_call | solution.py:257
  53.4 0.0 copy-done.9
  53.4 0.0 copy-done.10
  53.4 6.9 %collective-permute-done.2.refs_2_ = bf16[168,1536]{1,0:T(8,128)(2,1)S(1)} collective-permute-done((bf16[168,1536]{1,0:T(8,128)(2,1)S(1)}, bf16[168,1536]{1,0:T(8,128)(2,1)S(1)}, u32[]{:S(2)}, u32[]{:S(2)}) %collective-permute-start.2) | collective-permute-done | bytes 516128 | tf_op jit(solution)/shard_map/ppermute | solution.py:271
  60.3 0.0 all-to-all-done.1.own_ref
  60.3 0.0 copy-start.1
  60.4 2.1 %collective-permute-start.3 = (bf16[4,192,640]{2,1,0:T(8,128)(2,1)S(1)}, bf16[4,192,640]{2,1,0:T(8,128)(2,1)S(1)}, u32[]{:S(2)}, u32[]{:S(2)}) collective-permute-start(bf16[4,192,640]{2,1,0:T(8,128)(2,1)S(1)} %all-to-all-done.1.own_ref), channel_id=1, source_target_pairs={{0,16},{16,0},{32,48},{48,32},{64,80},{80,64},{96,112},{112,96},{1... | collective-permute-start | bytes 2949128 | tf_op jit(solution)/shard_map/ppermute | solution.py:275
  62.4 2.5 %collective-permute-done.3.other_ref = bf16[4,192,640]{2,1,0:T(8,128)(2,1)S(1)} collective-permute-done((bf16[4,192,640]{2,1,0:T(8,128)(2,1)S(1)}, bf16[4,192,640]{2,1,0:T(8,128)(2,1)S(1)}, u32[]{:S(2)}, u32[]{:S(2)}) %collective-permute-start.3) | collective-permute-done | bytes 983072 | tf_op jit(solution)/shard_map/ppermute | solution.py:275
  65.0 0.0 copy-done.7
  65.0 0.9 copy-done.8
  65.9 5.9 %shard_map.77 = bf16[4,168,640]{2,1,0:T(8,128)(2,1)} custom-call(s32[3]{0:T(128)} %pad_add_fusion.place, bf16[4,192,640]{2,1,0:T(8,128)(2,1)} %copy-done.7, bf16[4,192,640]{2,1,0:T(8,128)(2,1)} %copy-done.8, bf16[168,1536]{1,0:T(8,128)(2,1)} %get-tuple-element.62.refs_0_, bf16[168,1536]{1,0:T(8,128)(2,1)} %copy-done.9, bf16[168,1536]{1,0:T(8,128)(2,1)} %copy-done.11, ...), custom_call_target="tpu_custom_call" | custom-call | tf_op jit(solution)/shard_map/pallas_call | solution.py:282
  71.8 4.7 %all-to-all-start.2 = ((bf16[4,168,640]{2,1,0:T(8,128)(2,1)}), bf16[4,168,640]{2,1,0:T(8,128)(2,1)S(1)}, u32[]{:S(2)}, u32[]{:S(2)}) async-start(bf16[4,168,640]{2,1,0:T(8,128)(2,1)} %shard_map.77), calls=%async_computation.2 | async-start | bytes 1720320 | tf_op jit(solution)/shard_map/all_to_all | solution.py:42
  76.5 3.8 %collective-permute-start.4 = (bf16[192,1344]{1,0:T(8,128)(2,1)}, bf16[192,1344]{1,0:T(8,128)(2,1)S(1)}, u32[]{:S(2)}, u32[]{:S(2)}) collective-permute-start(bf16[192,1344]{1,0:T(8,128)(2,1)} %get-tuple-element.71), channel_id=1, source_target_pairs={{0,128},{16,144},{32,160},{48,176},{64,192},{80,208},{96,224},{112... | collective-permute-start | bytes 1548296 | tf_op jit(solution)/shard_map/ppermute | solution.py:271
  80.3 3.4 %collective-permute-start.5 = (bf16[192,1344]{1,0:T(8,128)(2,1)S(1)}, bf16[192,1344]{1,0:T(8,128)(2,1)S(1)}, u32[]{:S(2)}, u32[]{:S(2)}) collective-permute-start(bf16[192,1344]{1,0:T(8,128)(2,1)S(1)} %copy-done.12), channel_id=1, source_target_pairs={{0,384},{16,400},{32,416},{48,432},{64,448},{80,464},{96,480},{112... | collective-permute-start | bytes 1548296 | tf_op jit(solution)/shard_map/ppermute | solution.py:271
  83.7 10.0 %collective-permute-done.4.refs_1_ = bf16[192,1344]{1,0:T(8,128)(2,1)S(1)} collective-permute-done((bf16[192,1344]{1,0:T(8,128)(2,1)}, bf16[192,1344]{1,0:T(8,128)(2,1)S(1)}, u32[]{:S(2)}, u32[]{:S(2)}) %collective-permute-start.4) | collective-permute-done | bytes 516128 | tf_op jit(solution)/shard_map/ppermute | solution.py:271
  93.7 2.0 %collective-permute-done.5.refs_3_ = bf16[192,1344]{1,0:T(8,128)(2,1)S(1)} collective-permute-done((bf16[192,1344]{1,0:T(8,128)(2,1)S(1)}, bf16[192,1344]{1,0:T(8,128)(2,1)S(1)}, u32[]{:S(2)}, u32[]{:S(2)}) %collective-permute-start.5) | collective-permute-done | bytes 516128 | tf_op jit(solution)/shard_map/ppermute | solution.py:271
  95.7 0.0 all-to-all-done.2.in_ref
  95.7 1.1 shard_map.78
  96.7 4.8 %all-to-all-start.3 = ((bf16[4,168,640]{2,1,0:T(8,128)(2,1)}), bf16[4,168,640]{2,1,0:T(8,128)(2,1)S(1)}, u32[]{:S(2)}, u32[]{:S(2)}) async-start(bf16[4,168,640]{2,1,0:T(8,128)(2,1)} %shard_map.78), calls=%async_computation.3 | async-start | bytes 1720320 | tf_op jit(solution)/shard_map/all_to_all | solution.py:42
  101.5 4.6 %collective-permute-start.6 = (bf16[192,1344]{1,0:T(8,128)(2,1)}, bf16[192,1344]{1,0:T(8,128)(2,1)S(1)}, u32[]{:S(2)}, u32[]{:S(2)}) collective-permute-start(bf16[192,1344]{1,0:T(8,128)(2,1)} %get-tuple-element.76), channel_id=1, source_target_pairs={{0,256},{16,272},{32,288},{48,304},{64,320},{80,336},{96,352},{112... | collective-permute-start | bytes 1548296 | tf_op jit(solution)/shard_map/ppermute | solution.py:271
  106.1 11.0 %collective-permute-done.6.refs_2_ = bf16[192,1344]{1,0:T(8,128)(2,1)S(1)} collective-permute-done((bf16[192,1344]{1,0:T(8,128)(2,1)}, bf16[192,1344]{1,0:T(8,128)(2,1)S(1)}, u32[]{:S(2)}, u32[]{:S(2)}) %collective-permute-start.6) | collective-permute-done | bytes 516128 | tf_op jit(solution)/shard_map/ppermute | solution.py:271
  117.1 0.0 all-to-all-done.3.own_ref
  117.1 1.9 %collective-permute-start.7 = (bf16[4,168,640]{2,1,0:T(8,128)(2,1)S(1)}, bf16[4,168,640]{2,1,0:T(8,128)(2,1)S(1)}, u32[]{:S(2)}, u32[]{:S(2)}) collective-permute-start(bf16[4,168,640]{2,1,0:T(8,128)(2,1)S(1)} %all-to-all-done.3.own_ref), channel_id=1, source_target_pairs={{0,16},{16,0},{32,48},{48,32},{64,80},{80,64},{96,112},{112,96},{1... | collective-permute-start | bytes 2580488 | tf_op jit(solution)/shard_map/ppermute | solution.py:275
  119.1 2.4 %collective-permute-done.7.other_ref = bf16[4,168,640]{2,1,0:T(8,128)(2,1)S(1)} collective-permute-done((bf16[4,168,640]{2,1,0:T(8,128)(2,1)S(1)}, bf16[4,168,640]{2,1,0:T(8,128)(2,1)S(1)}, u32[]{:S(2)}, u32[]{:S(2)}) %collective-permute-start.7) | collective-permute-done | bytes 860192 | tf_op jit(solution)/shard_map/ppermute | solution.py:275
  121.4 0.0 copy-done.3
  121.4 2.7 %shard_map.79 = bf16[4,192,640]{2,1,0:T(8,128)(2,1)S(1)} custom-call(s32[3]{0:T(128)S(1)} %copy-done.3, bf16[4,168,640]{2,1,0:T(8,128)(2,1)S(1)} %all-to-all-done.3.own_ref, bf16[4,168,640]{2,1,0:T(8,128)(2,1)S(1)} %collective-permute-done.7.other_ref, bf16[192,1344]{1,0:T(8,128)(2,1)S(1)} %copy-done, bf16[192,1344]{1,0:T(8,128)(2,1)S(1)} %collective-permute-done.4.refs_1_, ...), custom_call_target="tpu_custom_call" | custom-call | tf_op jit(solution)/shard_map/pallas_call | solution.py:282
  124.1 18.5 %all_to_all.30.in_ref = bf16[4,192,640]{2,1,0:T(8,128)(2,1)S(1)} all-to-all(bf16[4,192,640]{2,1,0:T(8,128)(2,1)S(1)} %shard_map.79), channel_id=1, replica_groups={{0,128,256,384},{16,144,272,400},{32,160,288,416},{48,176,304,432},{64,..., dimensions={0} | all-to-all | bytes 1966080 | tf_op jit(solution)/shard_map/all_to_all | solution.py:42
  142.6 0.3 shard_map.80
  143.0 29.0 %all_to_all.31.in_ref = bf16[16,64,128]{2,1,0:T(8,128)(2,1)S(1)} all-to-all(bf16[16,64,128]{2,1,0:T(8,128)(2,1)S(1)} %shard_map.80), channel_id=1, replica_groups=mesh['dp'=32,'expert'=16] {'expert'}, dimensions={0} | all-to-all | bytes 524288 | tf_op jit(solution)/shard_map/all_to_all | solution.py:330
  172.0 1.0 shard_map.81
  (16 shorter events, 0.0 us)
Async XLA Ops:
  0.0 4.0 %copy-start.6 = (s32[1,4]{1,0:T(1,128)S(1)}, s32[1,4]{1,0:T(1,128)}, u32[]{:S(2)}) copy-start(s32[1,4]{1,0:T(1,128)} %lengths.1) | copy-start | bytes 52
  0.0 4.0 %copy-start.5 = (f32[128,4]{0,1:T(4,128)S(1)}, f32[128,4]{0,1:T(4,128)}, u32[]{:S(2)}) copy-start(f32[128,4]{0,1:T(4,128)} %param.9) | copy-start | bytes 6148
  0.0 4.1 %copy-start.4 = (s32[128,4]{0,1:T(4,128)S(1)}, s32[128,4]{0,1:T(4,128)}, u32[]{:S(2)}) copy-start(s32[128,4]{0,1:T(4,128)} %param.8) | copy-start | bytes 6148
  0.0 4.1 %copy-start.2 = (bf16[128,192]{0,1:T(8,128)(2,1)S(1)}, bf16[128,192]{0,1:T(8,128)(2,1)}, u32[]{:S(2)}) copy-start(bf16[128,192]{0,1:T(8,128)(2,1)} %param.7) | copy-start | bytes 147460
  4.0 41.2 %copy-start.13 = (bf16[168,1536]{1,0:T(8,128)(2,1)S(1)}, bf16[168,1536]{1,0:T(8,128)(2,1)}, u32[]{:S(2)}) copy-start(bf16[168,1536]{1,0:T(8,128)(2,1)} %get-tuple-element.55) | copy-start | bytes 1548292
  5.9 33.7 %all-to-all-start = ((bf16[16,64,128]{2,1,0:T(8,128)(2,1)}), bf16[16,64,128]{2,1,0:T(8,128)(2,1)S(1)}, u32[]{:S(2)}, u32[]{:S(2)}) async-start(bf16[16,64,128]{2,1,0:T(8,128)(2,1)} %get-tuple-element.49), calls=%async_computation | async-start | bytes 524288 | tf_op jit(solution)/shard_map/all_to_all | solution.py:311
  21.1 15.3 %collective-permute-start = (bf16[168,1536]{1,0:T(8,128)(2,1)}, bf16[168,1536]{1,0:T(8,128)(2,1)S(1)}, u32[]{:S(2)}, u32[]{:S(2)}) collective-permute-start(bf16[168,1536]{1,0:T(8,128)(2,1)} %get-tuple-element.50), channel_id=1, source_target_pairs={{0,32},{16,48},{32,64},{48,80},{64,96},{80,112},{96,0},{112,16},{1... | collective-permute-start | bytes 1548296 | tf_op jit(solution)/shard_map/ppermute | solution.py:271
  24.6 15.0 %collective-permute-start.1 = (bf16[168,1536]{1,0:T(8,128)(2,1)}, bf16[168,1536]{1,0:T(8,128)(2,1)S(1)}, u32[]{:S(2)}, u32[]{:S(2)}) collective-permute-start(bf16[168,1536]{1,0:T(8,128)(2,1)} %get-tuple-element.51), channel_id=1, source_target_pairs={{0,96},{16,112},{32,0},{48,16},{64,32},{80,48},{96,64},{112,80},{1... | collective-permute-start | bytes 1548296 | tf_op jit(solution)/shard_map/ppermute | solution.py:271
  36.5 17.0 %copy-start.9 = (bf16[168,1536]{1,0:T(8,128)(2,1)}, bf16[168,1536]{1,0:T(8,128)(2,1)S(1)}, u32[]{:S(2)}) copy-start(bf16[168,1536]{1,0:T(8,128)(2,1)S(1)} %collective-permute-done.refs_1_) | copy-start | bytes 1548292
  39.7 13.8 %copy-start.10 = (bf16[168,1536]{1,0:T(8,128)(2,1)}, bf16[168,1536]{1,0:T(8,128)(2,1)S(1)}, u32[]{:S(2)}) copy-start(bf16[168,1536]{1,0:T(8,128)(2,1)S(1)} %collective-permute-done.1.refs_3_) | copy-start | bytes 1548292
  40.9 19.4 %all-to-all-start.1 = ((bf16[4,192,640]{2,1,0:T(8,128)(2,1)}), bf16[4,192,640]{2,1,0:T(8,128)(2,1)S(1)}, u32[]{:S(2)}, u32[]{:S(2)}) async-start(bf16[4,192,640]{2,1,0:T(8,128)(2,1)} %shard_map.75), calls=%async_computation.1 | async-start | bytes 1966080 | tf_op jit(solution)/shard_map/all_to_all | solution.py:42
  45.2 15.1 %collective-permute-start.2 = (bf16[168,1536]{1,0:T(8,128)(2,1)S(1)}, bf16[168,1536]{1,0:T(8,128)(2,1)S(1)}, u32[]{:S(2)}, u32[]{:S(2)}) collective-permute-start(bf16[168,1536]{1,0:T(8,128)(2,1)S(1)} %copy-done.13), channel_id=1, source_target_pairs={{0,64},{16,80},{32,96},{48,112},{64,0},{80,16},{96,32},{112,48},{1... | collective-permute-start | bytes 1548296 | tf_op jit(solution)/shard_map/ppermute | solution.py:271
  60.3 4.6 %copy-start.11 = (bf16[168,1536]{1,0:T(8,128)(2,1)}, bf16[168,1536]{1,0:T(8,128)(2,1)S(1)}, u32[]{:S(2)}) copy-start(bf16[168,1536]{1,0:T(8,128)(2,1)S(1)} %collective-permute-done.2.refs_2_) | copy-start | bytes 1548292
  60.3 4.6 %copy-start.7 = (bf16[4,192,640]{2,1,0:T(8,128)(2,1)}, bf16[4,192,640]{2,1,0:T(8,128)(2,1)S(1)}, u32[]{:S(2)}) copy-start(bf16[4,192,640]{2,1,0:T(8,128)(2,1)S(1)} %all-to-all-done.1.own_ref) | copy-start | bytes 2949124
  60.3 20.0 %copy-start.12 = (bf16[192,1344]{1,0:T(8,128)(2,1)S(1)}, bf16[192,1344]{1,0:T(8,128)(2,1)}, u32[]{:S(2)}) copy-start(bf16[192,1344]{1,0:T(8,128)(2,1)} %get-tuple-element.72) | copy-start | bytes 1548292
  60.3 35.3 %copy-start.1 = (bf16[1,640,168]{1,2,0:T(8,128)(2,1)S(1)}, bf16[1,640,168]{1,2,0:T(8,128)(2,1)}, u32[]{:S(2)}) copy-start(bf16[1,640,168]{1,2,0:T(8,128)(2,1)} %param.13) | copy-start | bytes 645124
  60.4 4.6 %collective-permute-start.3 = (bf16[4,192,640]{2,1,0:T(8,128)(2,1)S(1)}, bf16[4,192,640]{2,1,0:T(8,128)(2,1)S(1)}, u32[]{:S(2)}, u32[]{:S(2)}) collective-permute-start(bf16[4,192,640]{2,1,0:T(8,128)(2,1)S(1)} %all-to-all-done.1.own_ref), channel_id=1, source_target_pairs={{0,16},{16,0},{32,48},{48,32},{64,80},{80,64},{96,112},{112,96},{1... | collective-permute-start | bytes 2949128 | tf_op jit(solution)/shard_map/ppermute | solution.py:275
  65.0 0.9 copy-start.8
  71.8 23.9 %all-to-all-start.2 = ((bf16[4,168,640]{2,1,0:T(8,128)(2,1)}), bf16[4,168,640]{2,1,0:T(8,128)(2,1)S(1)}, u32[]{:S(2)}, u32[]{:S(2)}) async-start(bf16[4,168,640]{2,1,0:T(8,128)(2,1)} %shard_map.77), calls=%async_computation.2 | async-start | bytes 1720320 | tf_op jit(solution)/shard_map/all_to_all | solution.py:42
  76.5 44.9 %copy-start = (bf16[192,1344]{1,0:T(8,128)(2,1)S(1)}, bf16[192,1344]{1,0:T(8,128)(2,1)}, u32[]{:S(2)}) copy-start(bf16[192,1344]{1,0:T(8,128)(2,1)} %get-tuple-element.78.refs_0_) | copy-start | bytes 1548292
  76.5 44.9 %copy-start.3 = (s32[3]{0:T(128)S(1)}, s32[3]{0:T(128)}, u32[]{:S(2)}) copy-start(s32[3]{0:T(128)} %pad_add_fusion.place) | copy-start | bytes 40
  76.5 17.2 %collective-permute-start.4 = (bf16[192,1344]{1,0:T(8,128)(2,1)}, bf16[192,1344]{1,0:T(8,128)(2,1)S(1)}, u32[]{:S(2)}, u32[]{:S(2)}) collective-permute-start(bf16[192,1344]{1,0:T(8,128)(2,1)} %get-tuple-element.71), channel_id=1, source_target_pairs={{0,128},{16,144},{32,160},{48,176},{64,192},{80,208},{96,224},{112... | collective-permute-start | bytes 1548296 | tf_op jit(solution)/shard_map/ppermute | solution.py:271
  80.3 15.4 %collective-permute-start.5 = (bf16[192,1344]{1,0:T(8,128)(2,1)S(1)}, bf16[192,1344]{1,0:T(8,128)(2,1)S(1)}, u32[]{:S(2)}, u32[]{:S(2)}) collective-permute-start(bf16[192,1344]{1,0:T(8,128)(2,1)S(1)} %copy-done.12), channel_id=1, source_target_pairs={{0,384},{16,400},{32,416},{48,432},{64,448},{80,464},{96,480},{112... | collective-permute-start | bytes 1548296 | tf_op jit(solution)/shard_map/ppermute | solution.py:271
  96.7 20.4 %all-to-all-start.3 = ((bf16[4,168,640]{2,1,0:T(8,128)(2,1)}), bf16[4,168,640]{2,1,0:T(8,128)(2,1)S(1)}, u32[]{:S(2)}, u32[]{:S(2)}) async-start(bf16[4,168,640]{2,1,0:T(8,128)(2,1)} %shard_map.78), calls=%async_computation.3 | async-start | bytes 1720320 | tf_op jit(solution)/shard_map/all_to_all | solution.py:42
  101.5 15.6 %collective-permute-start.6 = (bf16[192,1344]{1,0:T(8,128)(2,1)}, bf16[192,1344]{1,0:T(8,128)(2,1)S(1)}, u32[]{:S(2)}, u32[]{:S(2)}) collective-permute-start(bf16[192,1344]{1,0:T(8,128)(2,1)} %get-tuple-element.76), channel_id=1, source_target_pairs={{0,256},{16,272},{32,288},{48,304},{64,320},{80,336},{96,352},{112... | collective-permute-start | bytes 1548296 | tf_op jit(solution)/shard_map/ppermute | solution.py:271
  117.1 4.3 %collective-permute-start.7 = (bf16[4,168,640]{2,1,0:T(8,128)(2,1)S(1)}, bf16[4,168,640]{2,1,0:T(8,128)(2,1)S(1)}, u32[]{:S(2)}, u32[]{:S(2)}) collective-permute-start(bf16[4,168,640]{2,1,0:T(8,128)(2,1)S(1)} %all-to-all-done.3.own_ref), channel_id=1, source_target_pairs={{0,16},{16,0},{32,48},{48,32},{64,80},{80,64},{96,112},{112,96},{1... | collective-permute-start | bytes 2580488 | tf_op jit(solution)/shard_map/ppermute | solution.py:275

commit v2 on v1

--- a/solution.py
+++ b/solution.py
@@ -40,6 +40,10 @@
 
 def exchange(blocks, groups):
     return lax.all_to_all(blocks, "dp", 0, 0, tiled=True, axis_index_groups=groups)
+
+
+def gather(block, groups):
+    return lax.all_gather(block, "dp", axis_index_groups=groups)
 
 
 def after(value, *others):
@@ -129,20 +133,11 @@
                 high = min((s + 1) * CAPACITY - b * LANES, LANES)
                 if low < high:
                     block = jnp.where((lane >= low) & (lane < high), turned[s], block)
-            block = block.astype(jnp.bfloat16)
-            for n in range(out_ref.shape[0]):
-                out_ref[n, q * chunk : (q + 1) * chunk, b * LANES : (b + 1) * LANES] = block
-
-
-def product_kernel(along, copied, place, own_ref, other_ref, *refs):
+            out_ref[q * chunk : (q + 1) * chunk, b * LANES : (b + 1) * LANES] = block.astype(jnp.bfloat16)
+
+
+def product_kernel(along, place, own_ref, other_ref, *refs):
     weights, out_ref, data = refs[:SIDE], refs[SIDE], refs[SIDE + 1]
-    copies = []
-    if copied:
-        held, sems = refs[SIDE + 2 : -1], refs[-1]
-        copies = [pltpu.make_async_copy(weights[k], held[k], sems.at[k]) for k in range(SIDE)]
-        weights = held
-    for copy in copies:
-        copy.start()
     deep = own_ref.shape[1]
     for core in range(CORES):
 
@@ -153,8 +148,6 @@
                 data[2 * n * deep : 2 * (n + 1) * deep, :] = jnp.concatenate([ref[n] for ref in both], axis=0)
 
     for k in range(SIDE):
-        if copied:
-            copies[k].wait()
         part = jnp.dot(weights[k][...], data[...], preferred_element_type=jnp.float32)
         out_ref[lax.rem(place[along] + SIDE - k, SIDE)] = part.astype(jnp.bfloat16)
 
@@ -167,9 +160,7 @@
 
 
 def gate_kernel(in_ref, gate_ref, out_ref):
-    hidden = (added(in_ref) * gate_ref[...].astype(jnp.float32)).astype(jnp.bfloat16)
-    for n in range(out_ref.shape[0]):
-        out_ref[n] = hidden
+    out_ref[...] = (added(in_ref) * gate_ref[...].astype(jnp.float32)).astype(jnp.bfloat16)
 
 
 def pack_kernel(in_ref, out_ref):
@@ -202,92 +193,81 @@
     out_ref[...] = total.astype(jnp.bfloat16)
 
 
-def cut_down_kernel(place, in_ref, *refs):
-    out_refs, held, into, out_of = refs[:SIDE], refs[SIDE : 2 * SIDE], refs[-2], refs[-1]
+def here():
+    me = lax.axis_index("dp")
+    return me // (SIDE * CORES), lax.rem(me // CORES, SIDE), lax.rem(me, CORES)
+
+
+def column_copies(ks, in_ref, out_refs, held, into, out_of):
     wide = in_ref.shape[1] // (SIDE * SIDE)
-
-    def taken(k, n):
-        block = n * SIDE + lax.rem(place[1] + k, SIDE)
-        return pltpu.make_async_copy(
-            in_ref.at[:, pl.ds(pl.multiple_of(block * wide, wide), wide)],
-            held[k].at[:, pl.ds(n * wide, wide)],
-            into.at[k, n],
-        )
-
-    def given(k):
-        return pltpu.make_async_copy(held[k], out_refs[k], out_of.at[k])
-
-    order = (1, 3, 2, 0)
-    for k in order:
+    taken, given = [], []
+    for k in ks:
         for n in range(SIDE):
-            taken(k, n).start()
-    for k in order:
-        for n in range(SIDE):
-            taken(k, n).wait()
-        given(k).start()
-    for k in order:
-        given(k).wait()
-
-
-def cut_up_kernel(place, in_ref, *refs):
-    out_refs, whole, held, into, out_of = refs[:SIDE], refs[SIDE], refs[SIDE + 1 : -2], refs[-2], refs[-1]
-    fetch = pltpu.make_async_copy(in_ref, whole, into)
+            block = n * SIDE + lax.rem(here()[1] + k, SIDE)
+            columns = pl.ds(pl.multiple_of(block * wide, wide), wide)
+            to = held[k].at[:, pl.ds(n * wide, wide)]
+            taken.append(pltpu.make_async_copy(in_ref.at[:, columns], to, into.at[len(taken)]))
+        given.append(pltpu.make_async_copy(held[k], out_refs[k], out_of.at[k]))
+    return taken, given
+
+
+def first_kernel(lengths, routes_ref, probs_ref, grad_ref, weights, out_ref, slot_ref, *refs):
+    parts, held, (into, out_of) = refs[: SIDE - 1], refs[SIDE - 1 : -2], refs[-2:]
+    taken, given = column_copies((1, 3, 2), weights, (None, *parts), (None, *held), into, out_of)
+    for copy in taken:
+        copy.start()
+    dispatch_kernel(lengths, routes_ref, probs_ref, grad_ref, out_ref, slot_ref)
+    for copy in taken:
+        copy.wait()
+    for copy in given:
+        copy.start()
+    for copy in given:
+        copy.wait()
+
+
+def second_kernel(up_ref, down_ref, *refs):
+    out_refs, kept_ref, whole, held, kept = refs[:SIDE], refs[SIDE], refs[SIDE + 1], refs[SIDE + 2 : -4], refs[-4]
+    fetched, into, out_of = refs[-3:]
+    fetch = pltpu.make_async_copy(up_ref, whole, fetched)
     fetch.start()
+    taken, given = column_copies((0,), down_ref, (kept_ref,), (kept,), into, out_of)
+    for copy in taken:
+        copy.start()
     fetch.wait()
-    wide = in_ref.shape[1] // SIDE
+    wide = up_ref.shape[1] // SIDE
     for at in range(SIDE):
 
-        @pl.when(place[0] == at)
+        @pl.when(here()[0] == at)
         def _(at=at):
             for k in range(SIDE):
                 n = (at + k) % SIDE
                 held[k][...] = whole[:, n * wide : (n + 1) * wide]
 
-    copies = [pltpu.make_async_copy(held[k], out_refs[k], out_of.at[k]) for k in range(SIDE)]
+    copies = [pltpu.make_async_copy(held[k], out_refs[k], out_of.at[k + 1]) for k in range(SIDE)]
     for copy in copies:
         copy.start()
-    for copy in copies:
+    for copy in taken:
         copy.wait()
-
-
-def cut(kernel, place, weights, whole, sems):
-    part = jax.ShapeDtypeStruct((weights.shape[0], weights.shape[1] // SIDE), weights.dtype)
-    in_hbm = pl.BlockSpec(memory_space=pltpu.HBM)
-    return list(
-        pl.pallas_call(
-            kernel,
-            out_shape=[part] * SIDE,
-            in_specs=[pl.BlockSpec(memory_space=pltpu.SMEM), in_hbm],
-            out_specs=[in_hbm] * SIDE,
-            scratch_shapes=[pltpu.VMEM(weights.shape, weights.dtype)] * whole
-            + [pltpu.VMEM(part.shape, part.dtype)] * SIDE
-            + [pltpu.SemaphoreType.DMA(shape) for shape in sems],
-            compiler_params=pltpu.CompilerParams(vmem_limit_bytes=MOST),
-        )(place, weights)
-    )
+    for copy in given:
+        copy.start()
+    for copy in copies + given:
+        copy.wait()
 
 
 def send(part, dx, dy):
     return lax.ppermute(part, "dp", moves(dx, dy))
 
 
-def product(along, copied, place, rows, weights):
+def product(along, place, rows, weights):
     other = lax.ppermute(rows, "dp", OTHER_CORE)
     _, deep, slots = rows.shape
-    in_vmem = pl.BlockSpec(memory_space=pltpu.VMEM)
-    scratch = [pltpu.VMEM((CORES * SIDE * deep, slots), jnp.bfloat16)]
-    if copied:
-        scratch += [pltpu.VMEM(part.shape, part.dtype) for part in weights]
-        scratch += [pltpu.SemaphoreType.DMA((SIDE,))]
-    return pl.pallas_call(
-        functools.partial(product_kernel, along, copied),
-        out_shape=jax.ShapeDtypeStruct((SIDE, weights[0].shape[0], slots), jnp.bfloat16),
-        in_specs=[pl.BlockSpec(memory_space=pltpu.SMEM)]
-        + [in_vmem] * 2
-        + [pl.BlockSpec(memory_space=pltpu.HBM) if copied else in_vmem] * SIDE,
-        out_specs=in_vmem,
-        scratch_shapes=scratch,
-        compiler_params=pltpu.CompilerParams(vmem_limit_bytes=MOST if copied else 12 * MIB),
+    return call(
+        functools.partial(product_kernel, along),
+        jax.ShapeDtypeStruct((SIDE, weights[0].shape[0], slots), jnp.bfloat16),
+        1,
+        2 + SIDE,
+        12 * MIB,
+        [pltpu.VMEM((CORES * SIDE * deep, slots), jnp.bfloat16)],
     )(place, rows, other, *weights)
 
 
@@ -295,37 +275,51 @@
     tokens, width = grad_out.shape
     hidden = w_down.shape[1]
     chunk = width // PIECES
-    me = lax.axis_index("dp")
-    place = jnp.stack([me // (SIDE * CORES), (me // CORES) % SIDE, me % CORES]).astype(jnp.int32)
+    place = jnp.stack(here()).astype(jnp.int32)
 
     def half(*shape):
         return jax.ShapeDtypeStruct(shape, jnp.bfloat16)
 
-    outgoing, slots = call(
-        dispatch_kernel, (half(EXPERTS, chunk, LANES), jax.ShapeDtypeStruct((EXPERTS, tokens), jnp.float32)), 1, 3
-    )(resp_len, routes.T, probs.T, grad_out.T)
     together = lax.optimization_barrier
-
-    down = cut(cut_down_kernel, place, w_down[0], 0, [(SIDE, SIDE), (SIDE,)])
-    outgoing, down = together((outgoing, down))
+    in_smem, in_vmem, in_hbm = (pl.BlockSpec(memory_space=m) for m in (pltpu.SMEM, pltpu.VMEM, pltpu.HBM))
+    deep, features = w_down.shape[1:]
+    part = half(deep, features // SIDE)
+    outgoing, slots, *down = pl.pallas_call(
+        first_kernel,
+        out_shape=[half(EXPERTS, chunk, LANES), jax.ShapeDtypeStruct((EXPERTS, tokens), jnp.float32)]
+        + [part] * (SIDE - 1),
+        in_specs=[in_smem] + [in_vmem] * 3 + [in_hbm],
+        out_specs=[in_vmem] * 2 + [in_hbm] * (SIDE - 1),
+        scratch_shapes=[pltpu.VMEM(part.shape, part.dtype)] * (SIDE - 1)
+        + [pltpu.SemaphoreType.DMA(((SIDE - 1) * SIDE,)), pltpu.SemaphoreType.DMA((SIDE,))],
+        compiler_params=pltpu.CompilerParams(vmem_limit_bytes=MOST),
+    )(resp_len, routes.T, probs.T, grad_out.T, w_down[0])
+
     arrived = lax.all_to_all(outgoing, "expert", 0, 0, tiled=True)
-    arrived, down[1], down[3] = together((arrived, send(down[1], 0, 1), send(down[3], 0, 3)))
-
-    spread = call(unpack_kernel, half(SIDE, width, SLOTS), 0, 1)(arrived)
-    spread, down[2], up = together((spread, down[2], w_up[0]))
-    rows = exchange(spread, X_GROUPS)
-    up = cut(cut_up_kernel, place, up, 1, [(), (SIDE,)])
-    rows, down[2], up = together((rows, send(down[2], 0, 2), up))
-
-    partial = product(1, True, place, rows, down)
+    up_part = half(width, w_up.shape[2] // SIDE)
+    *up, kept = pl.pallas_call(
+        second_kernel,
+        out_shape=[up_part] * SIDE + [part],
+        in_specs=[in_hbm] * 2,
+        out_specs=[in_hbm] * (SIDE + 1),
+        scratch_shapes=[pltpu.VMEM(w_up.shape[1:], w_up.dtype)]
+        + [pltpu.VMEM(up_part.shape, up_part.dtype)] * SIDE
+        + [pltpu.VMEM(part.shape, part.dtype)]
+        + [pltpu.SemaphoreType.DMA, pltpu.SemaphoreType.DMA((SIDE,)), pltpu.SemaphoreType.DMA((SIDE + 1,))],
+        compiler_params=pltpu.CompilerParams(vmem_limit_bytes=MOST),
+    )(after(w_up[0], outgoing), w_down[0])
+    down = [kept, *down]
+    arrived, up = together((arrived, up))
+    spread = call(unpack_kernel, half(width, SLOTS), 0, 1)(arrived)
+    rows = gather(spread, X_GROUPS)
+    rows, *down[1:] = together((rows, *[send(down[k], 0, k) for k in range(1, SIDE)]))
+    partial = product(1, place, rows, down)
+
     partial, up = together((partial, up))
-    sums = exchange(partial, Y_GROUPS)
-    sums, up[1], up[3] = together((sums, send(up[1], 1, 0), send(up[3], 3, 0)))
-    spread = call(gate_kernel, half(SIDE, hidden, SLOTS), 0, 2)(sums, gate_act[0].T)
-    spread, up[2] = together((spread, up[2]))
-    rows = exchange(spread, Y_GROUPS)
-    rows, up[2] = together((rows, send(up[2], 2, 0)))
-    partial = product(0, False, place, rows, up)
+    spread = call(gate_kernel, half(hidden, SLOTS), 0, 2)(exchange(partial, Y_GROUPS), gate_act[0].T)
+    rows = gather(spread, Y_GROUPS)
+    rows, up[1], up[3], up[2] = together((rows, *[send(up[k], k, 0) for k in (1, 3, 2)]))
+    partial = product(0, place, rows, up)
     returning = call(pack_kernel, half(EXPERTS, chunk, LANES), 0, 1)(exchange(partial, X_GROUPS))
     back = lax.all_to_all(returning, "expert", 0, 0, tiled=True)
     return call(combine_kernel, half(width, tokens), 0, 2)(back, slots).T

time: 174 us -> 151 us (0.87)
  waiting for transfers between devices: 47.4 us -> 14.7 us
  blocking collectives: 47.5 us -> 74 us
  starting transfers between devices: 54.7 us -> 44 us
  Pallas kernels: 21.5 us -> 15.8 us
    ppermute x6, waiting for transfers between devices: 42.5 us -> 3.46 us  [send(): return lax.ppermute(part, 'dp', moves(dx, dy))]
    all_gather x0 -> x2, blocking collectives: none -> 28.2 us  [gather(): return lax.all_gather(block, 'dp', axis_index_groups=groups)]
    all_to_all x3 -> x1, starting transfers between devices: 13.8 us -> 4.77 us  [exchange(): lax.all_to_all(blocks, 'dp', 0, 0, tiled=True, axis_index_groups=groups)]
    pallas_call x7 -> x6, Pallas kernels: 20.2 us -> 14.5 us  [the longest x2 6.17 us: product(): call(functools.partial(product_kernel, along), jax.ShapeDtypeStruct((SIDE...]
    all_to_all x1, waiting for transfers between devices: 0.01 us -> 4.1 us  [on_device(): arrived = lax.all_to_all(outgoing, 'expert', 0, 0, tiled=True)]
    all_to_all x1, blocking collectives: 29 us -> 26.5 us  [on_device(): back = lax.all_to_all(returning, 'expert', 0, 0, tiled=True)]
    all_to_all x3 -> x1, waiting for transfers between devices: 0.01 us -> 2.3 us  [exchange(): lax.all_to_all(blocks, 'dp', 0, 0, tiled=True, axis_index_groups=groups)]
  transfers between devices with their start and end apart: 12 -> 10, of which waited for: 8 -> 5; matrix products, arithmetic and copies ran while one was open for 0% -> 0% of each run, Pallas kernels for 2% -> 3%
where the time goes in v2:
time: 151 us
  blocking collectives  74 us (49%)
  starting transfers between devices  44 us (29%)
  Pallas kernels  15.8 us (10%)
  waiting for transfers between devices  14.7 us (10%)
  local copies, waits for them, and re-layouts  1.98 us (1%)
    all_gather x2, blocking collectives, gather(): return lax.all_gather(block, 'dp', axis_index_groups=groups)  28.2 us
    all_to_all x1, blocking collectives, on_device(): back = lax.all_to_all(returning, 'expert', 0, 0, tiled=True)  26.5 us
    ppermute x6, starting transfers between devices, send(): return lax.ppermute(part, 'dp', moves(dx, dy))  20.2 us
    all_to_all x1, blocking collectives, exchange(): lax.all_to_all(blocks, 'dp', 0, 0, tiled=True, axis_index_groups=groups)  19.3 us
    all_to_all x1, starting transfers between devices, on_device(): arrived = lax.all_to_all(outgoing, 'expert', 0, 0, tiled=True)  15.2 us
    pallas_call x2, Pallas kernels, product(): call(functools.partial(product_kernel, along), jax.ShapeDtypeStruct((SIDE...  6.17 us
    ppermute x2, waiting for transfers between devices, product(): other = lax.ppermute(rows, 'dp', OTHER_CORE)  4.78 us
    all_to_all x1, starting transfers between devices, exchange(): lax.all_to_all(blocks, 'dp', 0, 0, tiled=True, axis_index_groups=groups)  4.77 us
  transfers between devices with their start and end apart: 10, of which 5 were waited for; matrix products, arithmetic and copies ran while one was open for 0% of the time, Pallas kernels for 3%

profile of v2, /device:TPU:8, one launch (start us, length us, event | category | flops | bytes accessed | tf_op | source)
XLA Modules:
  0.0 150.7 jit_solution(6418376611874689727)
XLA Ops:
  0.0 4.3 %shard_map.73 = (bf16[16,64,128]{2,1,0:T(8,128)(2,1)}, f32[16,128]{1,0:T(8,128)}, bf16[168,1536]{1,0:T(8,128)(2,1)}, bf16[168,1536]{1,0:T(8,128)(2,1)}, bf16[168,1536]{1,0:T(8,128)(2,1)}) custom-call(s32[1,4]{1,0:T(1,128)} %lengths.1, s32[4,128]{1,0:T(4,128)} %bitcast.23, f32[4,128]{1,0:T(4,128)} %bitcast.24, bf16[192,128]{1,0:T(8,128)(2,1)} %bitcast.22, ...), custom_call_target="tpu_custom_call" | custom-call | tf_op jit(solution)/shard_map/pallas_call | solution.py:287
  4.4 15.2 %all-to-all-start = ((bf16[16,64,128]{2,1,0:T(8,128)(2,1)}), bf16[16,64,128]{2,1,0:T(8,128)(2,1)S(1)}, u32[]{:S(2)}, u32[]{:S(2)}) async-start(bf16[16,64,128]{2,1,0:T(8,128)(2,1)} %get-tuple-element.34), calls=%async_computation | async-start | bytes 524288 | tf_op jit(solution)/shard_map/all_to_all | solution.py:298
  19.6 3.5 %collective-permute-start = (bf16[168,1536]{1,0:T(8,128)(2,1)}, bf16[168,1536]{1,0:T(8,128)(2,1)S(1)}, u32[]{:S(2)}, u32[]{:S(2)}) collective-permute-start(bf16[168,1536]{1,0:T(8,128)(2,1)} %get-tuple-element.41), channel_id=1, source_target_pairs={{0,32},{16,48},{32,64},{48,80},{64,96},{80,112},{96,0},{112,16},{1... | collective-permute-start | bytes 1548296 | tf_op jit(solution)/shard_map/ppermute | solution.py:258
  23.1 2.8 %collective-permute-start.1 = (bf16[168,1536]{1,0:T(8,128)(2,1)}, bf16[168,1536]{1,0:T(8,128)(2,1)S(1)}, u32[]{:S(2)}, u32[]{:S(2)}) collective-permute-start(bf16[168,1536]{1,0:T(8,128)(2,1)} %get-tuple-element.42), channel_id=1, source_target_pairs={{0,64},{16,80},{32,96},{48,112},{64,0},{80,16},{96,32},{112,48},{1... | collective-permute-start | bytes 1548296 | tf_op jit(solution)/shard_map/ppermute | solution.py:258
  25.9 4.3 %collective-permute-start.2 = (bf16[168,1536]{1,0:T(8,128)(2,1)}, bf16[168,1536]{1,0:T(8,128)(2,1)S(1)}, u32[]{:S(2)}, u32[]{:S(2)}) collective-permute-start(bf16[168,1536]{1,0:T(8,128)(2,1)} %get-tuple-element.43), channel_id=1, source_target_pairs={{0,96},{16,112},{32,0},{48,16},{64,32},{80,48},{96,64},{112,80},{1... | collective-permute-start | bytes 1548296 | tf_op jit(solution)/shard_map/ppermute | solution.py:258
  30.2 3.6 %shard_map.74 = (bf16[192,1344]{1,0:T(8,128)(2,1)}, bf16[192,1344]{1,0:T(8,128)(2,1)}, bf16[192,1344]{1,0:T(8,128)(2,1)}, bf16[192,1344]{1,0:T(8,128)(2,1)}, bf16[168,1536]{1,0:T(8,128)(2,1)}) custom-call(bf16[192,5376]{1,0:T(8,128)(2,1)} %bitcast.21, bf16[168,6144]{1,0:T(8,128)(2,1)} %bitcast.20), custom_call_target="tpu_custom_call" | custom-call | tf_op jit(solution)/shard_map/pallas_call | solution.py:300
  33.8 4.1 %all-to-all-done.in_ref = bf16[16,64,128]{2,1,0:T(8,128)(2,1)S(1)} async-done(((bf16[16,64,128]{2,1,0:T(8,128)(2,1)}), bf16[16,64,128]{2,1,0:T(8,128)(2,1)S(1)}, u32[]{:S(2)}, u32[]{:S(2)}) %all-to-all-start) | async-done | bytes 262176 | tf_op jit(solution)/shard_map/all_to_all | solution.py:298
  37.9 0.3 shard_map.75
  38.2 14.7 %all-gather = bf16[768,640]{1,0:T(8,128)(2,1)S(1)} all-gather(bf16[192,640]{1,0:T(8,128)(2,1)S(1)} %shard_map.75), channel_id=2, replica_groups={{0,128,256,384},{16,144,272,400},{32,160,288,416},{48,176,304,432},{64,..., dimensions={0}, use_global_device_ids=true | all-gather | bytes 1228800 | tf_op jit(solution)/shard_map/all_gather | solution.py:46
  52.9 0.0 collective-permute-done.refs_1_
  52.9 0.0 collective-permute-done.1.refs_2_
  52.9 0.0 collective-permute-done.2.refs_3_
  52.9 1.9 %collective-permute-start.3 = (bf16[4,192,640]{2,1,0:T(8,128)(2,1)S(1)}, bf16[4,192,640]{2,1,0:T(8,128)(2,1)S(1)}, u32[]{:S(2)}, u32[]{:S(2)}) collective-permute-start(bf16[4,192,640]{2,1,0:T(8,128)(2,1)S(1)} %bitcast.14), channel_id=1, source_target_pairs={{0,16},{16,0},{32,48},{48,32},{64,80},{80,64},{96,112},{112,96},{1... | collective-permute-start | bytes 2949128 | tf_op jit(solution)/shard_map/ppermute | solution.py:262
  54.8 0.1 pad_add_fusion.place
  54.9 2.4 %collective-permute-done.3.other_ref = bf16[4,192,640]{2,1,0:T(8,128)(2,1)S(1)} collective-permute-done((bf16[4,192,640]{2,1,0:T(8,128)(2,1)S(1)}, bf16[4,192,640]{2,1,0:T(8,128)(2,1)S(1)}, u32[]{:S(2)}, u32[]{:S(2)}) %collective-permute-start.3) | collective-permute-done | bytes 983072 | tf_op jit(solution)/shard_map/ppermute | solution.py:262
  57.3 0.0 copy-start.1
  57.3 1.0 copy-done.1
  58.4 3.5 %shard_map.76 = bf16[4,168,640]{2,1,0:T(8,128)(2,1)} custom-call(s32[3]{0:T(128)S(1)} %pad_add_fusion.place, bf16[4,192,640]{2,1,0:T(8,128)(2,1)S(1)} %bitcast.15, bf16[4,192,640]{2,1,0:T(8,128)(2,1)S(1)} %collective-permute-done.3.other_ref, bf16[168,1536]{1,0:T(8,128)(2,1)S(1)} %copy-done.1, bf16[168,1536]{1,0:T(8,128)(2,1)S(1)} %collective-permute-done.refs_1_, ...), custom_call_target="tpu_custom_call" | custom-call | tf_op jit(solution)/shard_map/pallas_call | solution.py:264
  61.9 0.0 copy-start
  61.9 4.8 %all-to-all-start.1 = ((bf16[4,168,640]{2,1,0:T(8,128)(2,1)}), bf16[4,168,640]{2,1,0:T(8,128)(2,1)S(1)}, u32[]{:S(2)}, u32[]{:S(2)}) async-start(bf16[4,168,640]{2,1,0:T(8,128)(2,1)} %shard_map.76), calls=%async_computation.1 | async-start | bytes 1720320 | tf_op jit(solution)/shard_map/all_to_all | solution.py:42
  66.6 3.1 %collective-permute-start.4 = (bf16[192,1344]{1,0:T(8,128)(2,1)}, bf16[192,1344]{1,0:T(8,128)(2,1)S(1)}, u32[]{:S(2)}, u32[]{:S(2)}) collective-permute-start(bf16[192,1344]{1,0:T(8,128)(2,1)} %get-tuple-element.54), channel_id=1, source_target_pairs={{0,128},{16,144},{32,160},{48,176},{64,192},{80,208},{96,224},{112... | collective-permute-start | bytes 1548296 | tf_op jit(solution)/shard_map/ppermute | solution.py:258
  69.7 3.9 %collective-permute-start.5 = (bf16[192,1344]{1,0:T(8,128)(2,1)}, bf16[192,1344]{1,0:T(8,128)(2,1)S(1)}, u32[]{:S(2)}, u32[]{:S(2)}) collective-permute-start(bf16[192,1344]{1,0:T(8,128)(2,1)} %get-tuple-element.55), channel_id=1, source_target_pairs={{0,384},{16,400},{32,416},{48,432},{64,448},{80,464},{96,480},{112... | collective-permute-start | bytes 1548296 | tf_op jit(solution)/shard_map/ppermute | solution.py:258
  73.7 2.6 %collective-permute-start.6 = (bf16[192,1344]{1,0:T(8,128)(2,1)}, bf16[192,1344]{1,0:T(8,128)(2,1)S(1)}, u32[]{:S(2)}, u32[]{:S(2)}) collective-permute-start(bf16[192,1344]{1,0:T(8,128)(2,1)} %get-tuple-element.56), channel_id=1, source_target_pairs={{0,256},{16,272},{32,288},{48,304},{64,320},{80,336},{96,352},{112... | collective-permute-start | bytes 1548296 | tf_op jit(solution)/shard_map/ppermute | solution.py:258
  76.2 2.3 %all-to-all-done.1.in_ref = bf16[4,168,640]{2,1,0:T(8,128)(2,1)S(1)} async-done(((bf16[4,168,640]{2,1,0:T(8,128)(2,1)}), bf16[4,168,640]{2,1,0:T(8,128)(2,1)S(1)}, u32[]{:S(2)}, u32[]{:S(2)}) %all-to-all-start.1) | async-done | bytes 860192 | tf_op jit(solution)/shard_map/all_to_all | solution.py:42
  78.5 0.0 copy-start.2
  78.6 0.9 copy-done.2
  79.5 0.1 shard_map.77
  79.6 13.5 %all-gather.1 = bf16[672,640]{1,0:T(8,128)(2,1)S(1)} all-gather(bf16[168,640]{1,0:T(8,128)(2,1)S(1)} %shard_map.77), channel_id=3, replica_groups={{0,32,64,96},{16,48,80,112},{128,160,192,224},{144,176,208,240},{256,28..., dimensions={0}, use_global_device_ids=true | all-gather | bytes 1075200 | tf_op jit(solution)/shard_map/all_gather | solution.py:46
  93.1 0.0 collective-permute-done.4.refs_1_
  93.1 3.4 %collective-permute-done.5.refs_3_ = bf16[192,1344]{1,0:T(8,128)(2,1)S(1)} collective-permute-done((bf16[192,1344]{1,0:T(8,128)(2,1)}, bf16[192,1344]{1,0:T(8,128)(2,1)S(1)}, u32[]{:S(2)}, u32[]{:S(2)}) %collective-permute-start.5) | collective-permute-done | bytes 516128 | tf_op jit(solution)/shard_map/ppermute | solution.py:258
  96.6 0.0 collective-permute-done.6.refs_2_
  96.6 1.9 %collective-permute-start.7 = (bf16[4,168,640]{2,1,0:T(8,128)(2,1)S(1)}, bf16[4,168,640]{2,1,0:T(8,128)(2,1)S(1)}, u32[]{:S(2)}, u32[]{:S(2)}) collective-permute-start(bf16[4,168,640]{2,1,0:T(8,128)(2,1)S(1)} %bitcast.16), channel_id=1, source_target_pairs={{0,16},{16,0},{32,48},{48,32},{64,80},{80,64},{96,112},{112,96},{1... | collective-permute-start | bytes 2580488 | tf_op jit(solution)/shard_map/ppermute | solution.py:262
  98.5 2.4 %collective-permute-done.7.other_ref = bf16[4,168,640]{2,1,0:T(8,128)(2,1)S(1)} collective-permute-done((bf16[4,168,640]{2,1,0:T(8,128)(2,1)S(1)}, bf16[4,168,640]{2,1,0:T(8,128)(2,1)S(1)}, u32[]{:S(2)}, u32[]{:S(2)}) %collective-permute-start.7) | collective-permute-done | bytes 860192 | tf_op jit(solution)/shard_map/ppermute | solution.py:262
  100.9 0.0 copy-done
  100.9 2.7 %shard_map.78 = bf16[4,192,640]{2,1,0:T(8,128)(2,1)S(1)} custom-call(s32[3]{0:T(128)S(1)} %pad_add_fusion.place, bf16[4,168,640]{2,1,0:T(8,128)(2,1)S(1)} %bitcast.17, bf16[4,168,640]{2,1,0:T(8,128)(2,1)S(1)} %collective-permute-done.7.other_ref, bf16[192,1344]{1,0:T(8,128)(2,1)S(1)} %copy-done, bf16[192,1344]{1,0:T(8,128)(2,1)S(1)} %collective-permute-done.4.refs_1_, ...), custom_call_target="tpu_custom_call" | custom-call | tf_op jit(solution)/shard_map/pallas_call | solution.py:264
  103.6 0.0 copy-start.3
  103.6 19.3 %all_to_all.20.in_ref = bf16[4,192,640]{2,1,0:T(8,128)(2,1)S(1)} all-to-all(bf16[4,192,640]{2,1,0:T(8,128)(2,1)S(1)} %shard_map.78), channel_id=1, replica_groups={{0,128,256,384},{16,144,272,400},{32,160,288,416},{48,176,304,432},{64,..., dimensions={0} | all-to-all | bytes 1966080 | tf_op jit(solution)/shard_map/all_to_all | solution.py:42
  122.9 0.3 shard_map.79
  123.2 26.5 %all_to_all.21.in_ref = bf16[16,64,128]{2,1,0:T(8,128)(2,1)S(1)} all-to-all(bf16[16,64,128]{2,1,0:T(8,128)(2,1)S(1)} %shard_map.79), channel_id=1, replica_groups=mesh['dp'=32,'expert'=16] {'expert'}, dimensions={0} | all-to-all | bytes 524288 | tf_op jit(solution)/shard_map/all_to_all | solution.py:324
  149.7 0.0 copy-done.3
  149.7 1.0 shard_map.80
Async XLA Ops:
  4.4 33.6 %all-to-all-start = ((bf16[16,64,128]{2,1,0:T(8,128)(2,1)}), bf16[16,64,128]{2,1,0:T(8,128)(2,1)S(1)}, u32[]{:S(2)}, u32[]{:S(2)}) async-start(bf16[16,64,128]{2,1,0:T(8,128)(2,1)} %get-tuple-element.34), calls=%async_computation | async-start | bytes 524288 | tf_op jit(solution)/shard_map/all_to_all | solution.py:298
  19.6 33.3 %collective-permute-start = (bf16[168,1536]{1,0:T(8,128)(2,1)}, bf16[168,1536]{1,0:T(8,128)(2,1)S(1)}, u32[]{:S(2)}, u32[]{:S(2)}) collective-permute-start(bf16[168,1536]{1,0:T(8,128)(2,1)} %get-tuple-element.41), channel_id=1, source_target_pairs={{0,32},{16,48},{32,64},{48,80},{64,96},{80,112},{96,0},{112,16},{1... | collective-permute-start | bytes 1548296 | tf_op jit(solution)/shard_map/ppermute | solution.py:258
  23.1 29.8 %collective-permute-start.1 = (bf16[168,1536]{1,0:T(8,128)(2,1)}, bf16[168,1536]{1,0:T(8,128)(2,1)S(1)}, u32[]{:S(2)}, u32[]{:S(2)}) collective-permute-start(bf16[168,1536]{1,0:T(8,128)(2,1)} %get-tuple-element.42), channel_id=1, source_target_pairs={{0,64},{16,80},{32,96},{48,112},{64,0},{80,16},{96,32},{112,48},{1... | collective-permute-start | bytes 1548296 | tf_op jit(solution)/shard_map/ppermute | solution.py:258
  25.9 27.0 %collective-permute-start.2 = (bf16[168,1536]{1,0:T(8,128)(2,1)}, bf16[168,1536]{1,0:T(8,128)(2,1)S(1)}, u32[]{:S(2)}, u32[]{:S(2)}) collective-permute-start(bf16[168,1536]{1,0:T(8,128)(2,1)} %get-tuple-element.43), channel_id=1, source_target_pairs={{0,96},{16,112},{32,0},{48,16},{64,32},{80,48},{96,64},{112,80},{1... | collective-permute-start | bytes 1548296 | tf_op jit(solution)/shard_map/ppermute | solution.py:258
  52.9 4.5 %collective-permute-start.3 = (bf16[4,192,640]{2,1,0:T(8,128)(2,1)S(1)}, bf16[4,192,640]{2,1,0:T(8,128)(2,1)S(1)}, u32[]{:S(2)}, u32[]{:S(2)}) collective-permute-start(bf16[4,192,640]{2,1,0:T(8,128)(2,1)S(1)} %bitcast.14), channel_id=1, source_target_pairs={{0,16},{16,0},{32,48},{48,32},{64,80},{80,64},{96,112},{112,96},{1... | collective-permute-start | bytes 2949128 | tf_op jit(solution)/shard_map/ppermute | solution.py:262
  57.3 1.0 copy-start.1
  61.9 39.0 %copy-start = (bf16[192,1344]{1,0:T(8,128)(2,1)S(1)}, bf16[192,1344]{1,0:T(8,128)(2,1)}, u32[]{:S(2)}) copy-start(bf16[192,1344]{1,0:T(8,128)(2,1)} %get-tuple-element.58.refs_0_) | copy-start | bytes 1548292
  61.9 16.7 %all-to-all-start.1 = ((bf16[4,168,640]{2,1,0:T(8,128)(2,1)}), bf16[4,168,640]{2,1,0:T(8,128)(2,1)S(1)}, u32[]{:S(2)}, u32[]{:S(2)}) async-start(bf16[4,168,640]{2,1,0:T(8,128)(2,1)} %shard_map.76), calls=%async_computation.1 | async-start | bytes 1720320 | tf_op jit(solution)/shard_map/all_to_all | solution.py:42
  66.6 26.5 %collective-permute-start.4 = (bf16[192,1344]{1,0:T(8,128)(2,1)}, bf16[192,1344]{1,0:T(8,128)(2,1)S(1)}, u32[]{:S(2)}, u32[]{:S(2)}) collective-permute-start(bf16[192,1344]{1,0:T(8,128)(2,1)} %get-tuple-element.54), channel_id=1, source_target_pairs={{0,128},{16,144},{32,160},{48,176},{64,192},{80,208},{96,224},{112... | collective-permute-start | bytes 1548296 | tf_op jit(solution)/shard_map/ppermute | solution.py:258
  69.7 26.9 %collective-permute-start.5 = (bf16[192,1344]{1,0:T(8,128)(2,1)}, bf16[192,1344]{1,0:T(8,128)(2,1)S(1)}, u32[]{:S(2)}, u32[]{:S(2)}) collective-permute-start(bf16[192,1344]{1,0:T(8,128)(2,1)} %get-tuple-element.55), channel_id=1, source_target_pairs={{0,384},{16,400},{32,416},{48,432},{64,448},{80,464},{96,480},{112... | collective-permute-start | bytes 1548296 | tf_op jit(solution)/shard_map/ppermute | solution.py:258
  73.7 22.9 %collective-permute-start.6 = (bf16[192,1344]{1,0:T(8,128)(2,1)}, bf16[192,1344]{1,0:T(8,128)(2,1)S(1)}, u32[]{:S(2)}, u32[]{:S(2)}) collective-permute-start(bf16[192,1344]{1,0:T(8,128)(2,1)} %get-tuple-element.56), channel_id=1, source_target_pairs={{0,256},{16,272},{32,288},{48,304},{64,320},{80,336},{96,352},{112... | collective-permute-start | bytes 1548296 | tf_op jit(solution)/shard_map/ppermute | solution.py:258
  78.5 0.9 copy-start.2
  96.6 4.3 %collective-permute-start.7 = (bf16[4,168,640]{2,1,0:T(8,128)(2,1)S(1)}, bf16[4,168,640]{2,1,0:T(8,128)(2,1)S(1)}, u32[]{:S(2)}, u32[]{:S(2)}) collective-permute-start(bf16[4,168,640]{2,1,0:T(8,128)(2,1)S(1)} %bitcast.16), channel_id=1, source_target_pairs={{0,16},{16,0},{32,48},{48,32},{64,80},{80,64},{96,112},{112,96},{1... | collective-permute-start | bytes 2580488 | tf_op jit(solution)/shard_map/ppermute | solution.py:262
  103.6 46.1 %copy-start.3 = (f32[16,128]{1,0:T(8,128)S(1)}, f32[16,128]{1,0:T(8,128)}, u32[]{:S(2)}) copy-start(f32[16,128]{1,0:T(8,128)} %get-tuple-element.62.slot_ref) | copy-start | bytes 24580

commit v3 on v2

--- a/solution.py
+++ b/solution.py
@@ -36,6 +36,7 @@
 
 
 OTHER_CORE = moves(0, 0, 1)
+FIRST = (2, 1, 3)
 
 
 def exchange(blocks, groups):
@@ -80,7 +81,7 @@
     return jnp.where(piece < PIECES, within, -2).astype(jnp.float32)
 
 
-def dispatch_kernel(lengths, routes_ref, probs_ref, grad_ref, out_ref, slot_ref):
+def dispatch_kernel(lengths, routes_ref, probs_ref, grad_ref, out_ref, slot_ref, at_expert):
     width, tokens = grad_ref.shape
     at = iota((1, tokens), 1)
     weight = jnp.zeros((1, tokens), jnp.float32)
@@ -108,6 +109,7 @@
     chunk = width // PIECES
     source = grad_ref[...].astype(jnp.float32)
     for e in range(EXPERTS):
+        at_expert(e)
         pick = jnp.where(slot[e : e + 1, :] == held, 1.0, 0.0).astype(jnp.bfloat16)
         scaled = (source * factor[e : e + 1, :]).astype(jnp.bfloat16)
         full = lax.dot_general(scaled, pick, (((1,), (1,)), ((), ())), preferred_element_type=jnp.float32)
@@ -198,68 +200,75 @@
     return me // (SIDE * CORES), lax.rem(me // CORES, SIDE), lax.rem(me, CORES)
 
 
-def column_copies(ks, in_ref, out_refs, held, into, out_of):
+def column_copies(ks, in_ref, held, sems):
     wide = in_ref.shape[1] // (SIDE * SIDE)
-    taken, given = [], []
-    for k in ks:
+    copies = []
+    for to, k in zip(held, ks):
         for n in range(SIDE):
             block = n * SIDE + lax.rem(here()[1] + k, SIDE)
             columns = pl.ds(pl.multiple_of(block * wide, wide), wide)
-            to = held[k].at[:, pl.ds(n * wide, wide)]
-            taken.append(pltpu.make_async_copy(in_ref.at[:, columns], to, into.at[len(taken)]))
-        given.append(pltpu.make_async_copy(held[k], out_refs[k], out_of.at[k]))
-    return taken, given
+            sem = sems.at[len(copies)]
+            copies.append(pltpu.make_async_copy(in_ref.at[:, columns], to.at[:, pl.ds(n * wide, wide)], sem))
+    return copies
 
 
 def first_kernel(lengths, routes_ref, probs_ref, grad_ref, weights, out_ref, slot_ref, *refs):
     parts, held, (into, out_of) = refs[: SIDE - 1], refs[SIDE - 1 : -2], refs[-2:]
-    taken, given = column_copies((1, 3, 2), weights, (None, *parts), (None, *held), into, out_of)
+    taken = column_copies(FIRST, weights, held, into)
+    given = [pltpu.make_async_copy(held[i], parts[i], out_of.at[i]) for i in range(SIDE - 1)]
     for copy in taken:
         copy.start()
-    dispatch_kernel(lengths, routes_ref, probs_ref, grad_ref, out_ref, slot_ref)
+
+    def pass_on(expert):
+        i = expert // SIDE - 1
+        if expert % SIDE == 0 and i >= 0:
+            for copy in taken[i * SIDE : (i + 1) * SIDE]:
+                copy.wait()
+            given[i].start()
+
+    dispatch_kernel(lengths, routes_ref, probs_ref, grad_ref, out_ref, slot_ref, pass_on)
+    for copy in given:
+        copy.wait()
+
+
+def cut_up_kernel(up_ref, down_ref, *refs):
+    out_refs, (kept_ref, windows, held, kept, fetched, out_of, into, kept_out) = refs[:SIDE], refs[SIDE:]
+    wide, window = held.shape[2], windows.shape[2]
+    fetches = []
+    for n in range(SIDE):
+        columns = pl.ds(n * wide // LANES * LANES, window)
+        fetches.append(pltpu.make_async_copy(up_ref.at[:, columns], windows.at[n], fetched.at[n]))
+    taken = column_copies((0,), down_ref, (kept,), into)
+    for copy in fetches + taken:
+        copy.start()
+    given = [[pltpu.make_async_copy(held.at[n], ref, out_of.at[n]) for ref in out_refs] for n in range(SIDE)]
+
+    def given_on(n, act):
+        for k in range(SIDE):
+
+            @pl.when(lax.rem(here()[0] + k, SIDE) == n)
+            def _(k=k):
+                act(given[n][k])
+
+    for n in range(SIDE):
+        fetches[n].wait()
+        skip = n * wide % LANES
+        held[n] = windows[n, :, skip : skip + wide]
+        given_on(n, lambda copy: copy.start())
     for copy in taken:
         copy.wait()
-    for copy in given:
-        copy.start()
-    for copy in given:
-        copy.wait()
-
-
-def second_kernel(up_ref, down_ref, *refs):
-    out_refs, kept_ref, whole, held, kept = refs[:SIDE], refs[SIDE], refs[SIDE + 1], refs[SIDE + 2 : -4], refs[-4]
-    fetched, into, out_of = refs[-3:]
-    fetch = pltpu.make_async_copy(up_ref, whole, fetched)
-    fetch.start()
-    taken, given = column_copies((0,), down_ref, (kept_ref,), (kept,), into, out_of)
-    for copy in taken:
-        copy.start()
-    fetch.wait()
-    wide = up_ref.shape[1] // SIDE
-    for at in range(SIDE):
-
-        @pl.when(here()[0] == at)
-        def _(at=at):
-            for k in range(SIDE):
-                n = (at + k) % SIDE
-                held[k][...] = whole[:, n * wide : (n + 1) * wide]
-
-    copies = [pltpu.make_async_copy(held[k], out_refs[k], out_of.at[k + 1]) for k in range(SIDE)]
-    for copy in copies:
-        copy.start()
-    for copy in taken:
-        copy.wait()
-    for copy in given:
-        copy.start()
-    for copy in copies + given:
-        copy.wait()
+    last = pltpu.make_async_copy(kept, kept_ref, kept_out)
+    last.start()
+    for n in range(SIDE):
+        given_on(n, lambda copy: copy.wait())
+    last.wait()
 
 
 def send(part, dx, dy):
     return lax.ppermute(part, "dp", moves(dx, dy))
 
 
-def product(along, place, rows, weights):
-    other = lax.ppermute(rows, "dp", OTHER_CORE)
+def product(along, place, rows, other, weights):
     _, deep, slots = rows.shape
     return call(
         functools.partial(product_kernel, along),
@@ -291,35 +300,40 @@
         in_specs=[in_smem] + [in_vmem] * 3 + [in_hbm],
         out_specs=[in_vmem] * 2 + [in_hbm] * (SIDE - 1),
         scratch_shapes=[pltpu.VMEM(part.shape, part.dtype)] * (SIDE - 1)
-        + [pltpu.SemaphoreType.DMA(((SIDE - 1) * SIDE,)), pltpu.SemaphoreType.DMA((SIDE,))],
+        + [pltpu.SemaphoreType.DMA(((SIDE - 1) * SIDE,)), pltpu.SemaphoreType.DMA((SIDE - 1,))],
         compiler_params=pltpu.CompilerParams(vmem_limit_bytes=MOST),
     )(resp_len, routes.T, probs.T, grad_out.T, w_down[0])
 
     arrived = lax.all_to_all(outgoing, "expert", 0, 0, tiled=True)
+    spread = call(unpack_kernel, half(width, SLOTS), 0, 1)(arrived)
+    rows = gather(spread, X_GROUPS)
+    rows, *down = together((rows, *[send(cut, 0, k) for k, cut in zip(FIRST, down)]))
+
     up_part = half(width, w_up.shape[2] // SIDE)
+    window = -(-(up_part.shape[1] + LANES // 2) // LANES) * LANES
     *up, kept = pl.pallas_call(
-        second_kernel,
+        cut_up_kernel,
         out_shape=[up_part] * SIDE + [part],
         in_specs=[in_hbm] * 2,
         out_specs=[in_hbm] * (SIDE + 1),
-        scratch_shapes=[pltpu.VMEM(w_up.shape[1:], w_up.dtype)]
-        + [pltpu.VMEM(up_part.shape, up_part.dtype)] * SIDE
-        + [pltpu.VMEM(part.shape, part.dtype)]
-        + [pltpu.SemaphoreType.DMA, pltpu.SemaphoreType.DMA((SIDE,)), pltpu.SemaphoreType.DMA((SIDE + 1,))],
+        scratch_shapes=[
+            pltpu.VMEM((SIDE, width, window), w_up.dtype),
+            pltpu.VMEM((SIDE, *up_part.shape), w_up.dtype),
+            pltpu.VMEM(part.shape, part.dtype),
+        ]
+        + [pltpu.SemaphoreType.DMA((SIDE,))] * 3
+        + [pltpu.SemaphoreType.DMA],
         compiler_params=pltpu.CompilerParams(vmem_limit_bytes=MOST),
-    )(after(w_up[0], outgoing), w_down[0])
-    down = [kept, *down]
-    arrived, up = together((arrived, up))
-    spread = call(unpack_kernel, half(width, SLOTS), 0, 1)(arrived)
-    rows = gather(spread, X_GROUPS)
-    rows, *down[1:] = together((rows, *[send(down[k], 0, k) for k in range(1, SIDE)]))
-    partial = product(1, place, rows, down)
+    )(after(w_up[0], rows), w_down[0])
+    down = dict(zip(FIRST, down))
+    partial = product(1, place, rows, lax.ppermute(rows, "dp", OTHER_CORE), [kept, *[down[k] for k in range(1, SIDE)]])
 
     partial, up = together((partial, up))
     spread = call(gate_kernel, half(hidden, SLOTS), 0, 2)(exchange(partial, Y_GROUPS), gate_act[0].T)
     rows = gather(spread, Y_GROUPS)
-    rows, up[1], up[3], up[2] = together((rows, *[send(up[k], k, 0) for k in (1, 3, 2)]))
-    partial = product(0, place, rows, up)
+    rows, *sent = together((rows, *[send(up[k], k, 0) for k in FIRST]))
+    up = [up[0]] + [sent[FIRST.index(k)] for k in range(1, SIDE)]
+    partial = product(0, place, rows, lax.ppermute(rows, "dp", OTHER_CORE), up)
     returning = call(pack_kernel, half(EXPERTS, chunk, LANES), 0, 1)(exchange(partial, X_GROUPS))
     back = lax.all_to_all(returning, "expert", 0, 0, tiled=True)
     return call(combine_kernel, half(width, tokens), 0, 2)(back, slots).T

time: 151 us -> 148 us (0.980)
  blocking collectives: 74 us -> 70.1 us
    all_to_all x1, waiting for transfers between devices: 4.1 us -> 8.3 us  [on_device(): arrived = lax.all_to_all(outgoing, 'expert', 0, 0, tiled=True)]
    ppermute x2, waiting for transfers between devices: 4.78 us -> 2.35 us  [the longest x1 2.35 us: on_device(): partial = product(0, place, rows, lax.ppermute(rows, 'dp', OTHER_CORE), up)]
    all_to_all x1, blocking collectives: 26.5 us -> 24.8 us  [on_device(): back = lax.all_to_all(returning, 'expert', 0, 0, tiled=True)]
  transfers between devices with their start and end apart: 10 -> 10, of which waited for: 5 -> 4; matrix products, arithmetic and copies ran while one was open for 0% -> 0% of each run, Pallas kernels for 3% -> 2%
where the time goes in v3:
time: 148 us; the launch traced here: 147 us
  blocking collectives  70.1 us (47%)
  starting transfers between devices  44.7 us (30%)
  waiting for transfers between devices  15.6 us (11%)
  Pallas kernels  14.8 us (10%)
  local copies, waits for them, and re-layouts  1.98 us (1%)
    all_gather x2, blocking collectives, gather(): return lax.all_gather(block, 'dp', axis_index_groups=groups)  27.1 us
    all_to_all x1, blocking collectives, on_device(): back = lax.all_to_all(returning, 'expert', 0, 0, tiled=True)  24.8 us
    ppermute x6, starting transfers between devices, send(): return lax.ppermute(part, 'dp', moves(dx, dy))  20.5 us
    all_to_all x1, blocking collectives, exchange(): lax.all_to_all(blocks, 'dp', 0, 0, tiled=True, axis_index_groups=groups)  18.2 us
    all_to_all x1, starting transfers between devices, on_device(): arrived = lax.all_to_all(outgoing, 'expert', 0, 0, tiled=True)  15.2 us
    all_to_all x1, waiting for transfers between devices, on_device(): arrived = lax.all_to_all(outgoing, 'expert', 0, 0, tiled=True)  8.3 us
    pallas_call x2, Pallas kernels, product(): call(functools.partial(product_kernel, along), jax.ShapeDtypeStruct((SIDE...  6.13 us
    all_to_all x1, starting transfers between devices, exchange(): lax.all_to_all(blocks, 'dp', 0, 0, tiled=True, axis_index_groups=groups)  5.16 us
  transfers between devices with their start and end apart: 10, of which 4 were waited for; matrix products, arithmetic and copies ran while one was open for 0% of the time, Pallas kernels for 2%

profile of v3, /device:TPU:8, one launch (start us, length us, event | category | flops | bytes accessed | tf_op | source)
XLA Modules:
  0.0 147.3 jit_solution(6850494328711139936)
XLA Ops:
  0.0 4.1 %shard_map.73 = (bf16[16,64,128]{2,1,0:T(8,128)(2,1)}, f32[16,128]{1,0:T(8,128)}, bf16[168,1536]{1,0:T(8,128)(2,1)}, bf16[168,1536]{1,0:T(8,128)(2,1)}, bf16[168,1536]{1,0:T(8,128)(2,1)}) custom-call(s32[1,4]{1,0:T(1,128)} %lengths.1, s32[4,128]{1,0:T(4,128)} %bitcast.23, f32[4,128]{1,0:T(4,128)} %bitcast.24, bf16[192,128]{1,0:T(8,128)(2,1)} %bitcast.22, ...), custom_call_target="tpu_custom_call" | custom-call | tf_op jit(solution)/shard_map/pallas_call | solution.py:296
  4.1 15.2 %all-to-all-start = ((bf16[16,64,128]{2,1,0:T(8,128)(2,1)}), bf16[16,64,128]{2,1,0:T(8,128)(2,1)S(1)}, u32[]{:S(2)}, u32[]{:S(2)}) async-start(bf16[16,64,128]{2,1,0:T(8,128)(2,1)} %get-tuple-element.29), calls=%async_computation | async-start | bytes 524288 | tf_op jit(solution)/shard_map/all_to_all | solution.py:307
  19.3 4.2 %collective-permute-start = (bf16[168,1536]{1,0:T(8,128)(2,1)}, bf16[168,1536]{1,0:T(8,128)(2,1)S(1)}, u32[]{:S(2)}, u32[]{:S(2)}) collective-permute-start(bf16[168,1536]{1,0:T(8,128)(2,1)} %get-tuple-element.30), channel_id=1, source_target_pairs={{0,64},{16,80},{32,96},{48,112},{64,0},{80,16},{96,32},{112,48},{1... | collective-permute-start | bytes 1548296 | tf_op jit(solution)/shard_map/ppermute | solution.py:268
  23.5 1.9 %collective-permute-start.1 = (bf16[168,1536]{1,0:T(8,128)(2,1)}, bf16[168,1536]{1,0:T(8,128)(2,1)S(1)}, u32[]{:S(2)}, u32[]{:S(2)}) collective-permute-start(bf16[168,1536]{1,0:T(8,128)(2,1)} %get-tuple-element.31), channel_id=1, source_target_pairs={{0,32},{16,48},{32,64},{48,80},{64,96},{80,112},{96,0},{112,16},{1... | collective-permute-start | bytes 1548296 | tf_op jit(solution)/shard_map/ppermute | solution.py:268
  25.4 3.9 %collective-permute-start.2 = (bf16[168,1536]{1,0:T(8,128)(2,1)}, bf16[168,1536]{1,0:T(8,128)(2,1)S(1)}, u32[]{:S(2)}, u32[]{:S(2)}) collective-permute-start(bf16[168,1536]{1,0:T(8,128)(2,1)} %get-tuple-element.32), channel_id=1, source_target_pairs={{0,96},{16,112},{32,0},{48,16},{64,32},{80,48},{96,64},{112,80},{1... | collective-permute-start | bytes 1548296 | tf_op jit(solution)/shard_map/ppermute | solution.py:268
  29.4 8.3 %all-to-all-done.in_ref = bf16[16,64,128]{2,1,0:T(8,128)(2,1)S(1)} async-done(((bf16[16,64,128]{2,1,0:T(8,128)(2,1)}), bf16[16,64,128]{2,1,0:T(8,128)(2,1)S(1)}, u32[]{:S(2)}, u32[]{:S(2)}) %all-to-all-start) | async-done | bytes 262176 | tf_op jit(solution)/shard_map/all_to_all | solution.py:307
  37.7 0.3 shard_map.74
  37.9 14.3 %all-gather = bf16[768,640]{1,0:T(8,128)(2,1)S(1)} all-gather(bf16[192,640]{1,0:T(8,128)(2,1)S(1)} %shard_map.74), channel_id=2, replica_groups={{0,128,256,384},{16,144,272,400},{32,160,288,416},{48,176,304,432},{64,..., dimensions={0}, use_global_device_ids=true | all-gather | bytes 1228800 | tf_op jit(solution)/shard_map/all_gather | solution.py:47
  52.2 0.0 collective-permute-done.refs_2_
  52.2 0.0 collective-permute-done.1.refs_1_
  52.2 0.0 collective-permute-done.2.refs_3_
  52.2 1.9 %collective-permute-start.3 = (bf16[4,192,640]{2,1,0:T(8,128)(2,1)S(1)}, bf16[4,192,640]{2,1,0:T(8,128)(2,1)S(1)}, u32[]{:S(2)}, u32[]{:S(2)}) collective-permute-start(bf16[4,192,640]{2,1,0:T(8,128)(2,1)S(1)} %bitcast.14), channel_id=1, source_target_pairs={{0,16},{16,0},{32,48},{48,32},{64,80},{80,64},{96,112},{112,96},{1... | collective-permute-start | bytes 2949128 | tf_op jit(solution)/shard_map/ppermute | solution.py:329
  54.2 0.1 pad_add_fusion.place
  54.2 2.9 %shard_map.75 = (bf16[192,1344]{1,0:T(8,128)(2,1)}, bf16[192,1344]{1,0:T(8,128)(2,1)}, bf16[192,1344]{1,0:T(8,128)(2,1)}, bf16[192,1344]{1,0:T(8,128)(2,1)}, bf16[168,1536]{1,0:T(8,128)(2,1)}) custom-call(bf16[192,5376]{1,0:T(8,128)(2,1)} %bitcast.21, bf16[168,6144]{1,0:T(8,128)(2,1)} %bitcast.20), custom_call_target="tpu_custom_call" | custom-call | tf_op jit(solution)/shard_map/pallas_call | solution.py:314
  57.1 0.0 collective-permute-done.3.other_ref
  57.1 0.0 copy-start.1
  57.1 1.0 copy-done.1
  58.2 3.5 %shard_map.76 = bf16[4,168,640]{2,1,0:T(8,128)(2,1)} custom-call(s32[3]{0:T(128)S(1)} %pad_add_fusion.place, bf16[4,192,640]{2,1,0:T(8,128)(2,1)S(1)} %bitcast.15, bf16[4,192,640]{2,1,0:T(8,128)(2,1)S(1)} %collective-permute-done.3.other_ref, bf16[168,1536]{1,0:T(8,128)(2,1)S(1)} %copy-done.1, bf16[168,1536]{1,0:T(8,128)(2,1)S(1)} %collective-permute-done.1.refs_1_, ...), custom_call_target="tpu_custom_call" | custom-call | tf_op jit(solution)/shard_map/pallas_call | solution.py:273
  61.7 0.0 copy-start
  61.7 5.2 %all-to-all-start.1 = ((bf16[4,168,640]{2,1,0:T(8,128)(2,1)}), bf16[4,168,640]{2,1,0:T(8,128)(2,1)S(1)}, u32[]{:S(2)}, u32[]{:S(2)}) async-start(bf16[4,168,640]{2,1,0:T(8,128)(2,1)} %shard_map.76), calls=%async_computation.1 | async-start | bytes 1720320 | tf_op jit(solution)/shard_map/all_to_all | solution.py:43
  66.8 3.4 %collective-permute-start.4 = (bf16[192,1344]{1,0:T(8,128)(2,1)}, bf16[192,1344]{1,0:T(8,128)(2,1)S(1)}, u32[]{:S(2)}, u32[]{:S(2)}) collective-permute-start(bf16[192,1344]{1,0:T(8,128)(2,1)} %get-tuple-element.44), channel_id=1, source_target_pairs={{0,256},{16,272},{32,288},{48,304},{64,320},{80,336},{96,352},{112... | collective-permute-start | bytes 1548296 | tf_op jit(solution)/shard_map/ppermute | solution.py:268
  70.2 3.7 %collective-permute-start.5 = (bf16[192,1344]{1,0:T(8,128)(2,1)}, bf16[192,1344]{1,0:T(8,128)(2,1)S(1)}, u32[]{:S(2)}, u32[]{:S(2)}) collective-permute-start(bf16[192,1344]{1,0:T(8,128)(2,1)} %get-tuple-element.45), channel_id=1, source_target_pairs={{0,128},{16,144},{32,160},{48,176},{64,192},{80,208},{96,224},{112... | collective-permute-start | bytes 1548296 | tf_op jit(solution)/shard_map/ppermute | solution.py:268
  73.9 3.4 %collective-permute-start.6 = (bf16[192,1344]{1,0:T(8,128)(2,1)}, bf16[192,1344]{1,0:T(8,128)(2,1)S(1)}, u32[]{:S(2)}, u32[]{:S(2)}) collective-permute-start(bf16[192,1344]{1,0:T(8,128)(2,1)} %get-tuple-element.46), channel_id=1, source_target_pairs={{0,384},{16,400},{32,416},{48,432},{64,448},{80,464},{96,480},{112... | collective-permute-start | bytes 1548296 | tf_op jit(solution)/shard_map/ppermute | solution.py:268
  77.3 1.8 %all-to-all-done.1.in_ref = bf16[4,168,640]{2,1,0:T(8,128)(2,1)S(1)} async-done(((bf16[4,168,640]{2,1,0:T(8,128)(2,1)}), bf16[4,168,640]{2,1,0:T(8,128)(2,1)S(1)}, u32[]{:S(2)}, u32[]{:S(2)}) %all-to-all-start.1) | async-done | bytes 860192 | tf_op jit(solution)/shard_map/all_to_all | solution.py:43
  79.1 0.0 copy-start.2
  79.1 0.9 copy-done.2
  80.0 0.2 shard_map.77
  80.2 12.9 %all-gather.1 = bf16[672,640]{1,0:T(8,128)(2,1)S(1)} all-gather(bf16[168,640]{1,0:T(8,128)(2,1)S(1)} %shard_map.77), channel_id=3, replica_groups={{0,32,64,96},{16,48,80,112},{128,160,192,224},{144,176,208,240},{256,28..., dimensions={0}, use_global_device_ids=true | all-gather | bytes 1075200 | tf_op jit(solution)/shard_map/all_gather | solution.py:47
  93.0 0.0 collective-permute-done.4.refs_2_
  93.0 3.1 %collective-permute-done.5.refs_1_ = bf16[192,1344]{1,0:T(8,128)(2,1)S(1)} collective-permute-done((bf16[192,1344]{1,0:T(8,128)(2,1)}, bf16[192,1344]{1,0:T(8,128)(2,1)S(1)}, u32[]{:S(2)}, u32[]{:S(2)}) %collective-permute-start.5) | collective-permute-done | bytes 516128 | tf_op jit(solution)/shard_map/ppermute | solution.py:268
  96.1 0.0 collective-permute-done.6.refs_3_
  96.1 1.9 %collective-permute-start.7 = (bf16[4,168,640]{2,1,0:T(8,128)(2,1)S(1)}, bf16[4,168,640]{2,1,0:T(8,128)(2,1)S(1)}, u32[]{:S(2)}, u32[]{:S(2)}) collective-permute-start(bf16[4,168,640]{2,1,0:T(8,128)(2,1)S(1)} %bitcast.16), channel_id=1, source_target_pairs={{0,16},{16,0},{32,48},{48,32},{64,80},{80,64},{96,112},{112,96},{1... | collective-permute-start | bytes 2580488 | tf_op jit(solution)/shard_map/ppermute | solution.py:336
  98.0 2.4 %collective-permute-done.7.other_ref = bf16[4,168,640]{2,1,0:T(8,128)(2,1)S(1)} collective-permute-done((bf16[4,168,640]{2,1,0:T(8,128)(2,1)S(1)}, bf16[4,168,640]{2,1,0:T(8,128)(2,1)S(1)}, u32[]{:S(2)}, u32[]{:S(2)}) %collective-permute-start.7) | collective-permute-done | bytes 860192 | tf_op jit(solution)/shard_map/ppermute | solution.py:336
  100.4 0.0 copy-done
  100.4 2.7 %shard_map.78 = bf16[4,192,640]{2,1,0:T(8,128)(2,1)S(1)} custom-call(s32[3]{0:T(128)S(1)} %pad_add_fusion.place, bf16[4,168,640]{2,1,0:T(8,128)(2,1)S(1)} %bitcast.17, bf16[4,168,640]{2,1,0:T(8,128)(2,1)S(1)} %collective-permute-done.7.other_ref, bf16[192,1344]{1,0:T(8,128)(2,1)S(1)} %copy-done, bf16[192,1344]{1,0:T(8,128)(2,1)S(1)} %collective-permute-done.5.refs_1_, ...), custom_call_target="tpu_custom_call" | custom-call | tf_op jit(solution)/shard_map/pallas_call | solution.py:273
  103.1 0.0 copy-start.3
  103.1 18.2 %all_to_all.20.in_ref = bf16[4,192,640]{2,1,0:T(8,128)(2,1)S(1)} all-to-all(bf16[4,192,640]{2,1,0:T(8,128)(2,1)S(1)} %shard_map.78), channel_id=1, replica_groups={{0,128,256,384},{16,144,272,400},{32,160,288,416},{48,176,304,432},{64,..., dimensions={0} | all-to-all | bytes 1966080 | tf_op jit(solution)/shard_map/all_to_all | solution.py:43
  121.2 0.3 shard_map.79
  121.5 24.8 %all_to_all.21.in_ref = bf16[16,64,128]{2,1,0:T(8,128)(2,1)S(1)} all-to-all(bf16[16,64,128]{2,1,0:T(8,128)(2,1)S(1)} %shard_map.79), channel_id=1, replica_groups=mesh['dp'=32,'expert'=16] {'expert'}, dimensions={0} | all-to-all | bytes 524288 | tf_op jit(solution)/shard_map/all_to_all | solution.py:338
  146.3 0.0 copy-done.3
  146.3 1.0 shard_map.80
Async XLA Ops:
  4.1 33.6 %all-to-all-start = ((bf16[16,64,128]{2,1,0:T(8,128)(2,1)}), bf16[16,64,128]{2,1,0:T(8,128)(2,1)S(1)}, u32[]{:S(2)}, u32[]{:S(2)}) async-start(bf16[16,64,128]{2,1,0:T(8,128)(2,1)} %get-tuple-element.29), calls=%async_computation | async-start | bytes 524288 | tf_op jit(solution)/shard_map/all_to_all | solution.py:307
  19.3 32.9 %collective-permute-start = (bf16[168,1536]{1,0:T(8,128)(2,1)}, bf16[168,1536]{1,0:T(8,128)(2,1)S(1)}, u32[]{:S(2)}, u32[]{:S(2)}) collective-permute-start(bf16[168,1536]{1,0:T(8,128)(2,1)} %get-tuple-element.30), channel_id=1, source_target_pairs={{0,64},{16,80},{32,96},{48,112},{64,0},{80,16},{96,32},{112,48},{1... | collective-permute-start | bytes 1548296 | tf_op jit(solution)/shard_map/ppermute | solution.py:268
  23.5 28.7 %collective-permute-start.1 = (bf16[168,1536]{1,0:T(8,128)(2,1)}, bf16[168,1536]{1,0:T(8,128)(2,1)S(1)}, u32[]{:S(2)}, u32[]{:S(2)}) collective-permute-start(bf16[168,1536]{1,0:T(8,128)(2,1)} %get-tuple-element.31), channel_id=1, source_target_pairs={{0,32},{16,48},{32,64},{48,80},{64,96},{80,112},{96,0},{112,16},{1... | collective-permute-start | bytes 1548296 | tf_op jit(solution)/shard_map/ppermute | solution.py:268
  25.4 26.8 %collective-permute-start.2 = (bf16[168,1536]{1,0:T(8,128)(2,1)}, bf16[168,1536]{1,0:T(8,128)(2,1)S(1)}, u32[]{:S(2)}, u32[]{:S(2)}) collective-permute-start(bf16[168,1536]{1,0:T(8,128)(2,1)} %get-tuple-element.32), channel_id=1, source_target_pairs={{0,96},{16,112},{32,0},{48,16},{64,32},{80,48},{96,64},{112,80},{1... | collective-permute-start | bytes 1548296 | tf_op jit(solution)/shard_map/ppermute | solution.py:268
  52.2 4.9 %collective-permute-start.3 = (bf16[4,192,640]{2,1,0:T(8,128)(2,1)S(1)}, bf16[4,192,640]{2,1,0:T(8,128)(2,1)S(1)}, u32[]{:S(2)}, u32[]{:S(2)}) collective-permute-start(bf16[4,192,640]{2,1,0:T(8,128)(2,1)S(1)} %bitcast.14), channel_id=1, source_target_pairs={{0,16},{16,0},{32,48},{48,32},{64,80},{80,64},{96,112},{112,96},{1... | collective-permute-start | bytes 2949128 | tf_op jit(solution)/shard_map/ppermute | solution.py:329
  57.1 1.0 copy-start.1
  61.7 38.7 %copy-start = (bf16[192,1344]{1,0:T(8,128)(2,1)S(1)}, bf16[192,1344]{1,0:T(8,128)(2,1)}, u32[]{:S(2)}) copy-start(bf16[192,1344]{1,0:T(8,128)(2,1)} %get-tuple-element.48.refs_0_) | copy-start | bytes 1548292
  61.7 17.4 %all-to-all-start.1 = ((bf16[4,168,640]{2,1,0:T(8,128)(2,1)}), bf16[4,168,640]{2,1,0:T(8,128)(2,1)S(1)}, u32[]{:S(2)}, u32[]{:S(2)}) async-start(bf16[4,168,640]{2,1,0:T(8,128)(2,1)} %shard_map.76), calls=%async_computation.1 | async-start | bytes 1720320 | tf_op jit(solution)/shard_map/all_to_all | solution.py:43
  66.8 26.2 %collective-permute-start.4 = (bf16[192,1344]{1,0:T(8,128)(2,1)}, bf16[192,1344]{1,0:T(8,128)(2,1)S(1)}, u32[]{:S(2)}, u32[]{:S(2)}) collective-permute-start(bf16[192,1344]{1,0:T(8,128)(2,1)} %get-tuple-element.44), channel_id=1, source_target_pairs={{0,256},{16,272},{32,288},{48,304},{64,320},{80,336},{96,352},{112... | collective-permute-start | bytes 1548296 | tf_op jit(solution)/shard_map/ppermute | solution.py:268
  70.2 25.9 %collective-permute-start.5 = (bf16[192,1344]{1,0:T(8,128)(2,1)}, bf16[192,1344]{1,0:T(8,128)(2,1)S(1)}, u32[]{:S(2)}, u32[]{:S(2)}) collective-permute-start(bf16[192,1344]{1,0:T(8,128)(2,1)} %get-tuple-element.45), channel_id=1, source_target_pairs={{0,128},{16,144},{32,160},{48,176},{64,192},{80,208},{96,224},{112... | collective-permute-start | bytes 1548296 | tf_op jit(solution)/shard_map/ppermute | solution.py:268
  73.9 22.2 %collective-permute-start.6 = (bf16[192,1344]{1,0:T(8,128)(2,1)}, bf16[192,1344]{1,0:T(8,128)(2,1)S(1)}, u32[]{:S(2)}, u32[]{:S(2)}) collective-permute-start(bf16[192,1344]{1,0:T(8,128)(2,1)} %get-tuple-element.46), channel_id=1, source_target_pairs={{0,384},{16,400},{32,416},{48,432},{64,448},{80,464},{96,480},{112... | collective-permute-start | bytes 1548296 | tf_op jit(solution)/shard_map/ppermute | solution.py:268
  79.1 0.9 copy-start.2
  96.1 4.3 %collective-permute-start.7 = (bf16[4,168,640]{2,1,0:T(8,128)(2,1)S(1)}, bf16[4,168,640]{2,1,0:T(8,128)(2,1)S(1)}, u32[]{:S(2)}, u32[]{:S(2)}) collective-permute-start(bf16[4,168,640]{2,1,0:T(8,128)(2,1)S(1)} %bitcast.16), channel_id=1, source_target_pairs={{0,16},{16,0},{32,48},{48,32},{64,80},{80,64},{96,112},{112,96},{1... | collective-permute-start | bytes 2580488 | tf_op jit(solution)/shard_map/ppermute | solution.py:336
  103.1 43.3 %copy-start.3 = (f32[16,128]{1,0:T(8,128)S(1)}, f32[16,128]{1,0:T(8,128)}, u32[]{:S(2)}) copy-start(f32[16,128]{1,0:T(8,128)} %get-tuple-element.52.slot_ref) | copy-start | bytes 24580

commit v4 on v3

--- a/solution.py
+++ b/solution.py
@@ -154,6 +154,23 @@
         out_ref[lax.rem(place[along] + SIDE - k, SIDE)] = part.astype(jnp.bfloat16)
 
 
+def part_kernel(weights, data_ref, out_ref):
+    out_ref[...] = jnp.dot(weights[...], data_ref[...], preferred_element_type=jnp.float32).astype(jnp.bfloat16)
+
+
+def first_part_kernel(place, own_ref, other_ref, weights, data_ref, out_ref):
+    deep = own_ref.shape[1]
+    for core in range(CORES):
+
+        @pl.when(place[2] == core)
+        def _(core=core):
+            both = (own_ref, other_ref) if core == 0 else (other_ref, own_ref)
+            for n in range(SIDE):
+                data_ref[2 * n * deep : 2 * (n + 1) * deep, :] = jnp.concatenate([ref[n] for ref in both], axis=0)
+
+    part_kernel(weights, data_ref, out_ref)
+
+
 def added(in_ref):
     total = in_ref[0].astype(jnp.float32)
     for n in range(1, in_ref.shape[0]):
@@ -165,9 +182,12 @@
     out_ref[...] = (added(in_ref) * gate_ref[...].astype(jnp.float32)).astype(jnp.bfloat16)
 
 
-def pack_kernel(in_ref, out_ref):
+def pack_kernel(*refs):
+    in_refs, out_ref = refs[:-1], refs[-1]
     shards, chunk, _ = out_ref.shape
-    total = added(in_ref)
+    total = in_refs[0][...].astype(jnp.float32)
+    for ref in in_refs[1:]:
+        total = total + ref[...].astype(jnp.float32)
     piece, _ = pieces((1, LANES))
     lane = iota((1, LANES), 1)
     for s in range(shards):
@@ -333,8 +353,17 @@
     rows = gather(spread, Y_GROUPS)
     rows, *sent = together((rows, *[send(up[k], k, 0) for k in FIRST]))
     up = [up[0]] + [sent[FIRST.index(k)] for k in range(1, SIDE)]
-    partial = product(0, place, rows, lax.ppermute(rows, "dp", OTHER_CORE), up)
-    returning = call(pack_kernel, half(EXPERTS, chunk, LANES), 0, 1)(exchange(partial, X_GROUPS))
+    other = lax.ppermute(rows, "dp", OTHER_CORE)
+    depth = CORES * SIDE * hidden
+    cost = dict(flops=2 * width * depth * SLOTS, moved=2 * depth * (width + SLOTS))
+    data, part_sent = call(first_part_kernel, [half(depth, SLOTS), half(width, SLOTS)], 1, 3, **cost)(
+        place, rows, other, up[FIRST[0]]
+    )
+    sums = [send(part_sent, -FIRST[0], 0)]
+    for k in (*FIRST[1:], 0):
+        done = call(part_kernel, half(width, SLOTS), 0, 2, **cost)(up[k], data)
+        sums.append(send(done, -k, 0) if k else done)
+    returning = call(pack_kernel, half(EXPERTS, chunk, LANES), 0, SIDE)(*sums)
     back = lax.all_to_all(returning, "expert", 0, 0, tiled=True)
     return call(combine_kernel, half(width, tokens), 0, 2)(back, slots).T
 

time: 148 us -> 147 us (level)
  the two profiles are of different devices: /device:TPU:8 before, /device:TPU:40 now
where the time goes in v4:
time: 147 us
  starting transfers between devices  54.3 us (37%)
  blocking collectives  51.5 us (35%)
  waiting for transfers between devices  23.3 us (16%)
  Pallas kernels  15.2 us (10%)
  local copies, waits for them, and re-layouts  1.98 us (1%)
    ppermute x9, starting transfers between devices, send(): return lax.ppermute(part, 'dp', moves(dx, dy))  30.3 us
    all_gather x2, blocking collectives, gather(): return lax.all_gather(block, 'dp', axis_index_groups=groups)  27.7 us
    all_to_all x1, blocking collectives, on_device(): back = lax.all_to_all(returning, 'expert', 0, 0, tiled=True)  23.8 us
    all_to_all x1, starting transfers between devices, on_device(): arrived = lax.all_to_all(outgoing, 'expert', 0, 0, tiled=True)  15.2 us
    ppermute x9, waiting for transfers between devices, send(): return lax.ppermute(part, 'dp', moves(dx, dy))  11.2 us
    all_to_all x1, waiting for transfers between devices, on_device(): arrived = lax.all_to_all(outgoing, 'expert', 0, 0, tiled=True)  7.86 us
    all_to_all x1, starting transfers between devices, exchange(): lax.all_to_all(blocks, 'dp', 0, 0, tiled=True, axis_index_groups=groups)  4.93 us
    pallas_call x1, Pallas kernels, on_device(): pl.pallas_call(first_kernel, out_shape=[half(EXPERTS, chunk, LANES), jax....  4.05 us
  transfers between devices with their start and end apart: 13, of which 8 were waited for; matrix products, arithmetic and copies ran while one was open for 0% of the time, Pallas kernels for 3%

profile of v4, /device:TPU:40, one launch (start us, length us, event | category | flops | bytes accessed | tf_op | source)
XLA Modules:
  0.0 146.6 jit_solution(7793618388498619942)
XLA Ops:
  0.0 4.0 %shard_map.73 = (bf16[16,64,128]{2,1,0:T(8,128)(2,1)}, f32[16,128]{1,0:T(8,128)}, bf16[168,1536]{1,0:T(8,128)(2,1)}, bf16[168,1536]{1,0:T(8,128)(2,1)}, bf16[168,1536]{1,0:T(8,128)(2,1)}) custom-call(s32[1,4]{1,0:T(1,128)} %lengths.1, s32[4,128]{1,0:T(4,128)} %bitcast.23, f32[4,128]{1,0:T(4,128)} %bitcast.24, bf16[192,128]{1,0:T(8,128)(2,1)} %bitcast.22, ...), custom_call_target="tpu_custom_call" | custom-call | tf_op jit(solution)/shard_map/pallas_call | solution.py:316
  4.1 15.2 %all-to-all-start = ((bf16[16,64,128]{2,1,0:T(8,128)(2,1)}), bf16[16,64,128]{2,1,0:T(8,128)(2,1)S(1)}, u32[]{:S(2)}, u32[]{:S(2)}) async-start(bf16[16,64,128]{2,1,0:T(8,128)(2,1)} %get-tuple-element.31), calls=%async_computation | async-start | bytes 524288 | tf_op jit(solution)/shard_map/all_to_all | solution.py:327
  19.3 4.2 %collective-permute-start = (bf16[168,1536]{1,0:T(8,128)(2,1)}, bf16[168,1536]{1,0:T(8,128)(2,1)S(1)}, u32[]{:S(2)}, u32[]{:S(2)}) collective-permute-start(bf16[168,1536]{1,0:T(8,128)(2,1)} %get-tuple-element.32), channel_id=1, source_target_pairs={{0,64},{16,80},{32,96},{48,112},{64,0},{80,16},{96,32},{112,48},{1... | collective-permute-start | bytes 1548296 | tf_op jit(solution)/shard_map/ppermute | solution.py:288
  23.5 1.9 %collective-permute-start.1 = (bf16[168,1536]{1,0:T(8,128)(2,1)}, bf16[168,1536]{1,0:T(8,128)(2,1)S(1)}, u32[]{:S(2)}, u32[]{:S(2)}) collective-permute-start(bf16[168,1536]{1,0:T(8,128)(2,1)} %get-tuple-element.33), channel_id=1, source_target_pairs={{0,32},{16,48},{32,64},{48,80},{64,96},{80,112},{96,0},{112,16},{1... | collective-permute-start | bytes 1548296 | tf_op jit(solution)/shard_map/ppermute | solution.py:288
  25.4 3.9 %collective-permute-start.2 = (bf16[168,1536]{1,0:T(8,128)(2,1)}, bf16[168,1536]{1,0:T(8,128)(2,1)S(1)}, u32[]{:S(2)}, u32[]{:S(2)}) collective-permute-start(bf16[168,1536]{1,0:T(8,128)(2,1)} %get-tuple-element.34), channel_id=1, source_target_pairs={{0,96},{16,112},{32,0},{48,16},{64,32},{80,48},{96,64},{112,80},{1... | collective-permute-start | bytes 1548296 | tf_op jit(solution)/shard_map/ppermute | solution.py:288
  29.3 7.9 %all-to-all-done.in_ref = bf16[16,64,128]{2,1,0:T(8,128)(2,1)S(1)} async-done(((bf16[16,64,128]{2,1,0:T(8,128)(2,1)}), bf16[16,64,128]{2,1,0:T(8,128)(2,1)S(1)}, u32[]{:S(2)}, u32[]{:S(2)}) %all-to-all-start) | async-done | bytes 262176 | tf_op jit(solution)/shard_map/all_to_all | solution.py:327
  37.2 0.3 shard_map.74
  37.5 14.8 %all-gather = bf16[768,640]{1,0:T(8,128)(2,1)S(1)} all-gather(bf16[192,640]{1,0:T(8,128)(2,1)S(1)} %shard_map.74), channel_id=2, replica_groups={{0,128,256,384},{16,144,272,400},{32,160,288,416},{48,176,304,432},{64,..., dimensions={0}, use_global_device_ids=true | all-gather | bytes 1228800 | tf_op jit(solution)/shard_map/all_gather | solution.py:47
  52.3 0.0 collective-permute-done.refs_2_
  52.3 0.0 collective-permute-done.1.refs_1_
  52.3 0.0 collective-permute-done.2.refs_3_
  52.3 1.9 %collective-permute-start.3 = (bf16[4,192,640]{2,1,0:T(8,128)(2,1)S(1)}, bf16[4,192,640]{2,1,0:T(8,128)(2,1)S(1)}, u32[]{:S(2)}, u32[]{:S(2)}) collective-permute-start(bf16[4,192,640]{2,1,0:T(8,128)(2,1)S(1)} %bitcast.14), channel_id=1, source_target_pairs={{0,16},{16,0},{32,48},{48,32},{64,80},{80,64},{96,112},{112,96},{1... | collective-permute-start | bytes 2949128 | tf_op jit(solution)/shard_map/ppermute | solution.py:349
  54.2 0.1 pad_add_fusion.place
  54.3 2.9 %shard_map.75 = (bf16[192,1344]{1,0:T(8,128)(2,1)}, bf16[192,1344]{1,0:T(8,128)(2,1)}, bf16[192,1344]{1,0:T(8,128)(2,1)}, bf16[192,1344]{1,0:T(8,128)(2,1)}, bf16[168,1536]{1,0:T(8,128)(2,1)}) custom-call(bf16[192,5376]{1,0:T(8,128)(2,1)} %bitcast.21, bf16[168,6144]{1,0:T(8,128)(2,1)} %bitcast.20), custom_call_target="tpu_custom_call" | custom-call | tf_op jit(solution)/shard_map/pallas_call | solution.py:334
  57.2 0.0 collective-permute-done.3.other_ref
  57.2 0.0 copy-start.1
  57.3 1.0 copy-done.1
  58.3 3.5 %shard_map.76 = bf16[4,168,640]{2,1,0:T(8,128)(2,1)} custom-call(s32[3]{0:T(128)S(1)} %pad_add_fusion.place, bf16[4,192,640]{2,1,0:T(8,128)(2,1)S(1)} %bitcast.15, bf16[4,192,640]{2,1,0:T(8,128)(2,1)S(1)} %collective-permute-done.3.other_ref, bf16[168,1536]{1,0:T(8,128)(2,1)S(1)} %copy-done.1, bf16[168,1536]{1,0:T(8,128)(2,1)S(1)} %collective-permute-done.1.refs_1_, ...), custom_call_target="tpu_custom_call" | custom-call | tf_op jit(solution)/shard_map/pallas_call | solution.py:293
  61.8 4.9 %all-to-all-start.1 = ((bf16[4,168,640]{2,1,0:T(8,128)(2,1)}), bf16[4,168,640]{2,1,0:T(8,128)(2,1)S(1)}, u32[]{:S(2)}, u32[]{:S(2)}) async-start(bf16[4,168,640]{2,1,0:T(8,128)(2,1)} %shard_map.76), calls=%async_computation.1 | async-start | bytes 1720320 | tf_op jit(solution)/shard_map/all_to_all | solution.py:43
  66.7 3.3 %collective-permute-start.4 = (bf16[192,1344]{1,0:T(8,128)(2,1)}, bf16[192,1344]{1,0:T(8,128)(2,1)S(1)}, u32[]{:S(2)}, u32[]{:S(2)}) collective-permute-start(bf16[192,1344]{1,0:T(8,128)(2,1)} %get-tuple-element.46), channel_id=1, source_target_pairs={{0,256},{16,272},{32,288},{48,304},{64,320},{80,336},{96,352},{112... | collective-permute-start | bytes 1548296 | tf_op jit(solution)/shard_map/ppermute | solution.py:288
  70.0 4.1 %collective-permute-start.5 = (bf16[192,1344]{1,0:T(8,128)(2,1)}, bf16[192,1344]{1,0:T(8,128)(2,1)S(1)}, u32[]{:S(2)}, u32[]{:S(2)}) collective-permute-start(bf16[192,1344]{1,0:T(8,128)(2,1)} %get-tuple-element.47), channel_id=1, source_target_pairs={{0,128},{16,144},{32,160},{48,176},{64,192},{80,208},{96,224},{112... | collective-permute-start | bytes 1548296 | tf_op jit(solution)/shard_map/ppermute | solution.py:288
  74.1 3.0 %collective-permute-start.6 = (bf16[192,1344]{1,0:T(8,128)(2,1)}, bf16[192,1344]{1,0:T(8,128)(2,1)S(1)}, u32[]{:S(2)}, u32[]{:S(2)}) collective-permute-start(bf16[192,1344]{1,0:T(8,128)(2,1)} %get-tuple-element.48), channel_id=1, source_target_pairs={{0,384},{16,400},{32,416},{48,432},{64,448},{80,464},{96,480},{112... | collective-permute-start | bytes 1548296 | tf_op jit(solution)/shard_map/ppermute | solution.py:288
  77.1 1.9 %all-to-all-done.1.in_ref = bf16[4,168,640]{2,1,0:T(8,128)(2,1)S(1)} async-done(((bf16[4,168,640]{2,1,0:T(8,128)(2,1)}), bf16[4,168,640]{2,1,0:T(8,128)(2,1)S(1)}, u32[]{:S(2)}, u32[]{:S(2)}) %all-to-all-start.1) | async-done | bytes 860192 | tf_op jit(solution)/shard_map/all_to_all | solution.py:43
  79.0 0.9 copy-done.2
  79.9 0.2 shard_map.77
  80.1 12.9 %all-gather.1 = bf16[672,640]{1,0:T(8,128)(2,1)S(1)} all-gather(bf16[168,640]{1,0:T(8,128)(2,1)S(1)} %shard_map.77), channel_id=3, replica_groups={{0,32,64,96},{16,48,80,112},{128,160,192,224},{144,176,208,240},{256,28..., dimensions={0}, use_global_device_ids=true | all-gather | bytes 1075200 | tf_op jit(solution)/shard_map/all_gather | solution.py:47
  92.9 0.0 collective-permute-done.4.weights
  92.9 3.1 %collective-permute-done.5.weights = bf16[192,1344]{1,0:T(8,128)(2,1)S(1)} collective-permute-done((bf16[192,1344]{1,0:T(8,128)(2,1)}, bf16[192,1344]{1,0:T(8,128)(2,1)S(1)}, u32[]{:S(2)}, u32[]{:S(2)}) %collective-permute-start.5) | collective-permute-done | bytes 516128 | tf_op jit(solution)/shard_map/ppermute | solution.py:288
  96.0 0.1 collective-permute-done.6.weights
  96.1 1.9 %collective-permute-start.7 = (bf16[4,168,640]{2,1,0:T(8,128)(2,1)S(1)}, bf16[4,168,640]{2,1,0:T(8,128)(2,1)S(1)}, u32[]{:S(2)}, u32[]{:S(2)}) collective-permute-start(bf16[4,168,640]{2,1,0:T(8,128)(2,1)S(1)} %bitcast.16), channel_id=1, source_target_pairs={{0,16},{16,0},{32,48},{48,32},{64,80},{80,64},{96,112},{112,96},{1... | collective-permute-start | bytes 2580488 | tf_op jit(solution)/shard_map/ppermute | solution.py:356
  98.0 2.4 %collective-permute-done.7.other_ref = bf16[4,168,640]{2,1,0:T(8,128)(2,1)S(1)} collective-permute-done((bf16[4,168,640]{2,1,0:T(8,128)(2,1)S(1)}, bf16[4,168,640]{2,1,0:T(8,128)(2,1)S(1)}, u32[]{:S(2)}, u32[]{:S(2)}) %collective-permute-start.7) | collective-permute-done | bytes 860192 | tf_op jit(solution)/shard_map/ppermute | solution.py:356
  100.4 1.3 shard_map.78
  101.7 0.0 copy-start
  101.7 0.6 shard_map.80
  102.3 0.6 shard_map.79
  102.9 0.0 copy-start.3
  102.9 4.0 %collective-permute-start.8 = (bf16[192,640]{1,0:T(8,128)(2,1)S(1)}, bf16[192,640]{1,0:T(8,128)(2,1)S(1)}, u32[]{:S(2)}, u32[]{:S(2)}) collective-permute-start(bf16[192,640]{1,0:T(8,128)(2,1)S(1)} %get-tuple-element.51), channel_id=1, source_target_pairs={{0,256},{16,272},{32,288},{48,304},{64,320},{80,336},{96,352},{112... | collective-permute-start | bytes 737288 | tf_op jit(solution)/shard_map/ppermute | solution.py:288
  106.9 3.9 %collective-permute-start.9 = (bf16[192,640]{1,0:T(8,128)(2,1)S(1)}, bf16[192,640]{1,0:T(8,128)(2,1)S(1)}, u32[]{:S(2)}, u32[]{:S(2)}) collective-permute-start(bf16[192,640]{1,0:T(8,128)(2,1)S(1)} %shard_map.79), channel_id=1, source_target_pairs={{0,384},{16,400},{32,416},{48,432},{64,448},{80,464},{96,480},{112... | collective-permute-start | bytes 737288 | tf_op jit(solution)/shard_map/ppermute | solution.py:288
  110.9 1.9 %collective-permute-start.10 = (bf16[192,640]{1,0:T(8,128)(2,1)S(1)}, bf16[192,640]{1,0:T(8,128)(2,1)S(1)}, u32[]{:S(2)}, u32[]{:S(2)}) collective-permute-start(bf16[192,640]{1,0:T(8,128)(2,1)S(1)} %shard_map.80), channel_id=1, source_target_pairs={{0,128},{16,144},{32,160},{48,176},{64,192},{80,208},{96,224},{112... | collective-permute-start | bytes 737288 | tf_op jit(solution)/shard_map/ppermute | solution.py:288
  112.8 0.0 copy-done
  112.8 0.6 shard_map.81.refs_3_
  113.4 0.9 collective-permute-done.8.refs_0_
  114.3 5.2 %collective-permute-done.9.refs_1_ = bf16[192,640]{1,0:T(8,128)(2,1)S(1)} collective-permute-done((bf16[192,640]{1,0:T(8,128)(2,1)S(1)}, bf16[192,640]{1,0:T(8,128)(2,1)S(1)}, u32[]{:S(2)}, u32[]{:S(2)}) %collective-permute-start.9) | collective-permute-done | bytes 245792 | tf_op jit(solution)/shard_map/ppermute | solution.py:288
  119.5 1.9 %collective-permute-done.10.refs_2_ = bf16[192,640]{1,0:T(8,128)(2,1)S(1)} collective-permute-done((bf16[192,640]{1,0:T(8,128)(2,1)S(1)}, bf16[192,640]{1,0:T(8,128)(2,1)S(1)}, u32[]{:S(2)}, u32[]{:S(2)}) %collective-permute-start.10) | collective-permute-done | bytes 245792 | tf_op jit(solution)/shard_map/ppermute | solution.py:288
  121.4 0.3 shard_map.82
  121.7 23.8 %all_to_all.15.in_ref = bf16[16,64,128]{2,1,0:T(8,128)(2,1)S(1)} all-to-all(bf16[16,64,128]{2,1,0:T(8,128)(2,1)S(1)} %shard_map.82), channel_id=1, replica_groups=mesh['dp'=32,'expert'=16] {'expert'}, dimensions={0} | all-to-all | bytes 524288 | tf_op jit(solution)/shard_map/all_to_all | solution.py:367
  145.6 0.0 copy-done.3
  145.6 1.0 shard_map.83
  (1 shorter events, 0.0 us)
Async XLA Ops:
  4.1 33.1 %all-to-all-start = ((bf16[16,64,128]{2,1,0:T(8,128)(2,1)}), bf16[16,64,128]{2,1,0:T(8,128)(2,1)S(1)}, u32[]{:S(2)}, u32[]{:S(2)}) async-start(bf16[16,64,128]{2,1,0:T(8,128)(2,1)} %get-tuple-element.31), calls=%async_computation | async-start | bytes 524288 | tf_op jit(solution)/shard_map/all_to_all | solution.py:327
  19.3 33.0 %collective-permute-start = (bf16[168,1536]{1,0:T(8,128)(2,1)}, bf16[168,1536]{1,0:T(8,128)(2,1)S(1)}, u32[]{:S(2)}, u32[]{:S(2)}) collective-permute-start(bf16[168,1536]{1,0:T(8,128)(2,1)} %get-tuple-element.32), channel_id=1, source_target_pairs={{0,64},{16,80},{32,96},{48,112},{64,0},{80,16},{96,32},{112,48},{1... | collective-permute-start | bytes 1548296 | tf_op jit(solution)/shard_map/ppermute | solution.py:288
  23.5 28.8 %collective-permute-start.1 = (bf16[168,1536]{1,0:T(8,128)(2,1)}, bf16[168,1536]{1,0:T(8,128)(2,1)S(1)}, u32[]{:S(2)}, u32[]{:S(2)}) collective-permute-start(bf16[168,1536]{1,0:T(8,128)(2,1)} %get-tuple-element.33), channel_id=1, source_target_pairs={{0,32},{16,48},{32,64},{48,80},{64,96},{80,112},{96,0},{112,16},{1... | collective-permute-start | bytes 1548296 | tf_op jit(solution)/shard_map/ppermute | solution.py:288
  25.4 26.9 %collective-permute-start.2 = (bf16[168,1536]{1,0:T(8,128)(2,1)}, bf16[168,1536]{1,0:T(8,128)(2,1)S(1)}, u32[]{:S(2)}, u32[]{:S(2)}) collective-permute-start(bf16[168,1536]{1,0:T(8,128)(2,1)} %get-tuple-element.34), channel_id=1, source_target_pairs={{0,96},{16,112},{32,0},{48,16},{64,32},{80,48},{96,64},{112,80},{1... | collective-permute-start | bytes 1548296 | tf_op jit(solution)/shard_map/ppermute | solution.py:288
  52.3 4.9 %collective-permute-start.3 = (bf16[4,192,640]{2,1,0:T(8,128)(2,1)S(1)}, bf16[4,192,640]{2,1,0:T(8,128)(2,1)S(1)}, u32[]{:S(2)}, u32[]{:S(2)}) collective-permute-start(bf16[4,192,640]{2,1,0:T(8,128)(2,1)S(1)} %bitcast.14), channel_id=1, source_target_pairs={{0,16},{16,0},{32,48},{48,32},{64,80},{80,64},{96,112},{112,96},{1... | collective-permute-start | bytes 2949128 | tf_op jit(solution)/shard_map/ppermute | solution.py:349
  57.2 1.0 copy-start.1
  61.8 17.2 %all-to-all-start.1 = ((bf16[4,168,640]{2,1,0:T(8,128)(2,1)}), bf16[4,168,640]{2,1,0:T(8,128)(2,1)S(1)}, u32[]{:S(2)}, u32[]{:S(2)}) async-start(bf16[4,168,640]{2,1,0:T(8,128)(2,1)} %shard_map.76), calls=%async_computation.1 | async-start | bytes 1720320 | tf_op jit(solution)/shard_map/all_to_all | solution.py:43
  66.7 26.2 %collective-permute-start.4 = (bf16[192,1344]{1,0:T(8,128)(2,1)}, bf16[192,1344]{1,0:T(8,128)(2,1)S(1)}, u32[]{:S(2)}, u32[]{:S(2)}) collective-permute-start(bf16[192,1344]{1,0:T(8,128)(2,1)} %get-tuple-element.46), channel_id=1, source_target_pairs={{0,256},{16,272},{32,288},{48,304},{64,320},{80,336},{96,352},{112... | collective-permute-start | bytes 1548296 | tf_op jit(solution)/shard_map/ppermute | solution.py:288
  70.0 25.9 %collective-permute-start.5 = (bf16[192,1344]{1,0:T(8,128)(2,1)}, bf16[192,1344]{1,0:T(8,128)(2,1)S(1)}, u32[]{:S(2)}, u32[]{:S(2)}) collective-permute-start(bf16[192,1344]{1,0:T(8,128)(2,1)} %get-tuple-element.47), channel_id=1, source_target_pairs={{0,128},{16,144},{32,160},{48,176},{64,192},{80,208},{96,224},{112... | collective-permute-start | bytes 1548296 | tf_op jit(solution)/shard_map/ppermute | solution.py:288
  74.1 22.0 %collective-permute-start.6 = (bf16[192,1344]{1,0:T(8,128)(2,1)}, bf16[192,1344]{1,0:T(8,128)(2,1)S(1)}, u32[]{:S(2)}, u32[]{:S(2)}) collective-permute-start(bf16[192,1344]{1,0:T(8,128)(2,1)} %get-tuple-element.48), channel_id=1, source_target_pairs={{0,384},{16,400},{32,416},{48,432},{64,448},{80,464},{96,480},{112... | collective-permute-start | bytes 1548296 | tf_op jit(solution)/shard_map/ppermute | solution.py:288
  79.0 0.9 copy-start.2
  96.1 4.3 %collective-permute-start.7 = (bf16[4,168,640]{2,1,0:T(8,128)(2,1)S(1)}, bf16[4,168,640]{2,1,0:T(8,128)(2,1)S(1)}, u32[]{:S(2)}, u32[]{:S(2)}) collective-permute-start(bf16[4,168,640]{2,1,0:T(8,128)(2,1)S(1)} %bitcast.16), channel_id=1, source_target_pairs={{0,16},{16,0},{32,48},{48,32},{64,80},{80,64},{96,112},{112,96},{1... | collective-permute-start | bytes 2580488 | tf_op jit(solution)/shard_map/ppermute | solution.py:356
  101.7 11.1 %copy-start = (bf16[192,1344]{1,0:T(8,128)(2,1)S(1)}, bf16[192,1344]{1,0:T(8,128)(2,1)}, u32[]{:S(2)}) copy-start(bf16[192,1344]{1,0:T(8,128)(2,1)} %get-tuple-element.55.weights) | copy-start | bytes 1548292
  102.9 42.7 %copy-start.3 = (f32[16,128]{1,0:T(8,128)S(1)}, f32[16,128]{1,0:T(8,128)}, u32[]{:S(2)}) copy-start(f32[16,128]{1,0:T(8,128)} %get-tuple-element.56.slot_ref) | copy-start | bytes 24580
  102.9 11.4 %collective-permute-start.8 = (bf16[192,640]{1,0:T(8,128)(2,1)S(1)}, bf16[192,640]{1,0:T(8,128)(2,1)S(1)}, u32[]{:S(2)}, u32[]{:S(2)}) collective-permute-start(bf16[192,640]{1,0:T(8,128)(2,1)S(1)} %get-tuple-element.51), channel_id=1, source_target_pairs={{0,256},{16,272},{32,288},{48,304},{64,320},{80,336},{96,352},{112... | collective-permute-start | bytes 737288 | tf_op jit(solution)/shard_map/ppermute | solution.py:288
  106.9 12.6 %collective-permute-start.9 = (bf16[192,640]{1,0:T(8,128)(2,1)S(1)}, bf16[192,640]{1,0:T(8,128)(2,1)S(1)}, u32[]{:S(2)}, u32[]{:S(2)}) collective-permute-start(bf16[192,640]{1,0:T(8,128)(2,1)S(1)} %shard_map.79), channel_id=1, source_target_pairs={{0,384},{16,400},{32,416},{48,432},{64,448},{80,464},{96,480},{112... | collective-permute-start | bytes 737288 | tf_op jit(solution)/shard_map/ppermute | solution.py:288
  110.9 10.5 %collective-permute-start.10 = (bf16[192,640]{1,0:T(8,128)(2,1)S(1)}, bf16[192,640]{1,0:T(8,128)(2,1)S(1)}, u32[]{:S(2)}, u32[]{:S(2)}) collective-permute-start(bf16[192,640]{1,0:T(8,128)(2,1)S(1)} %shard_map.80), channel_id=1, source_target_pairs={{0,128},{16,144},{32,160},{48,176},{64,192},{80,208},{96,224},{112... | collective-permute-start | bytes 737288 | tf_op jit(solution)/shard_map/ppermute | solution.py:288

commit v5 on v4

--- a/solution.py
+++ b/solution.py
@@ -158,7 +158,8 @@
     out_ref[...] = jnp.dot(weights[...], data_ref[...], preferred_element_type=jnp.float32).astype(jnp.bfloat16)
 
 
-def first_part_kernel(place, own_ref, other_ref, weights, data_ref, out_ref):
+def sent_parts_kernel(place, own_ref, other_ref, *refs):
+    weights, data_ref, out_refs = refs[: SIDE - 1], refs[SIDE - 1], refs[SIDE:]
     deep = own_ref.shape[1]
     for core in range(CORES):
 
@@ -168,7 +169,8 @@
             for n in range(SIDE):
                 data_ref[2 * n * deep : 2 * (n + 1) * deep, :] = jnp.concatenate([ref[n] for ref in both], axis=0)
 
-    part_kernel(weights, data_ref, out_ref)
+    for block, out_ref in zip(weights, out_refs):
+        part_kernel(block, data_ref, out_ref)
 
 
 def added(in_ref):
@@ -203,16 +205,17 @@
         out_ref[s] = block.astype(jnp.bfloat16)
 
 
-def combine_kernel(in_ref, slot_ref, out_ref):
+def combine_kernel(in_ref, slot_ref, out_ref, spread, picks):
     piece, _ = pieces((1, LANES))
     held = held_slots(slot_ref.shape[1])
-    total = jnp.zeros(out_ref.shape, jnp.float32)
+    chunk = in_ref.shape[1]
     for e in range(in_ref.shape[0]):
         block = in_ref[e].astype(jnp.float32)
-        spread = jnp.concatenate([jnp.where(piece == q, block, 0.0) for q in range(PIECES)], axis=0)
-        pick = jnp.where(slot_ref[e : e + 1, :] == held, 1.0, 0.0).astype(jnp.bfloat16)
-        total = total + jnp.dot(spread.astype(jnp.bfloat16), pick, preferred_element_type=jnp.float32)
-    out_ref[...] = total.astype(jnp.bfloat16)
+        lanes = slice(e * LANES, (e + 1) * LANES)
+        for q in range(PIECES):
+            spread[q * chunk : (q + 1) * chunk, lanes] = jnp.where(piece == q, block, 0.0).astype(jnp.bfloat16)
+        picks[lanes, :] = jnp.where(slot_ref[e : e + 1, :] == held, 1.0, 0.0).astype(jnp.bfloat16)
+    out_ref[...] = jnp.dot(spread[...], picks[...], preferred_element_type=jnp.float32).astype(jnp.bfloat16)
 
 
 def here():
@@ -356,16 +359,15 @@
     other = lax.ppermute(rows, "dp", OTHER_CORE)
     depth = CORES * SIDE * hidden
     cost = dict(flops=2 * width * depth * SLOTS, moved=2 * depth * (width + SLOTS))
-    data, part_sent = call(first_part_kernel, [half(depth, SLOTS), half(width, SLOTS)], 1, 3, **cost)(
-        place, rows, other, up[FIRST[0]]
+    data, *parts = call(sent_parts_kernel, [half(depth, SLOTS)] + [half(width, SLOTS)] * (SIDE - 1), 1, 1 + SIDE, 16 * MIB, **cost)(
+        place, rows, other, *[up[k] for k in FIRST]
     )
-    sums = [send(part_sent, -FIRST[0], 0)]
-    for k in (*FIRST[1:], 0):
-        done = call(part_kernel, half(width, SLOTS), 0, 2, **cost)(up[k], data)
-        sums.append(send(done, -k, 0) if k else done)
+    sums = [send(sent_part, -k, 0) for k, sent_part in zip(FIRST, parts)]
+    sums.append(call(part_kernel, half(width, SLOTS), 0, 2, **cost)(up[0], data))
     returning = call(pack_kernel, half(EXPERTS, chunk, LANES), 0, SIDE)(*sums)
     back = lax.all_to_all(returning, "expert", 0, 0, tiled=True)
-    return call(combine_kernel, half(width, tokens), 0, 2)(back, slots).T
+    scratch = [pltpu.VMEM((width, EXPERTS * LANES), jnp.bfloat16), pltpu.VMEM((EXPERTS * LANES, tokens), jnp.bfloat16)]
+    return call(combine_kernel, half(width, tokens), 0, 2, scratch=scratch)(back, slots).T
 
 
 def solution(mesh):

time: 147 us -> 147 us (level)
    pallas_call x5 -> x3, Pallas kernels: 4.06 us -> 3.89 us  [the longest x1 2.18 us: on_device(): call(sent_parts_kernel, [half(depth, SLOTS)] + [half(width, SLOTS)] * (SI...]
where the time goes in v5:
time: 147 us; the launch traced here: 146 us
  starting transfers between devices  54.3 us (37%)
  blocking collectives  51.7 us (35%)
  waiting for transfers between devices  23.1 us (16%)
  Pallas kernels  15.1 us (10%)
  local copies, waits for them, and re-layouts  1.98 us (1%)
    ppermute x9, starting transfers between devices, send(): return lax.ppermute(part, 'dp', moves(dx, dy))  30.3 us
    all_gather x2, blocking collectives, gather(): return lax.all_gather(block, 'dp', axis_index_groups=groups)  27.8 us
    all_to_all x1, blocking collectives, on_device(): back = lax.all_to_all(returning, 'expert', 0, 0, tiled=True)  23.8 us
    all_to_all x1, starting transfers between devices, on_device(): arrived = lax.all_to_all(outgoing, 'expert', 0, 0, tiled=True)  15.2 us
    ppermute x9, waiting for transfers between devices, send(): return lax.ppermute(part, 'dp', moves(dx, dy))  11 us
    all_to_all x1, waiting for transfers between devices, on_device(): arrived = lax.all_to_all(outgoing, 'expert', 0, 0, tiled=True)  7.86 us
    all_to_all x1, starting transfers between devices, exchange(): lax.all_to_all(blocks, 'dp', 0, 0, tiled=True, axis_index_groups=groups)  4.93 us
    pallas_call x1, Pallas kernels, on_device(): pl.pallas_call(first_kernel, out_shape=[half(EXPERTS, chunk, LANES), jax....  4.05 us
  transfers between devices with their start and end apart: 13, of which 8 were waited for; matrix products, arithmetic and copies ran while one was open for 0% of the time, Pallas kernels for 3%

profile of v5, /device:TPU:40, one launch (start us, length us, event | category | flops | bytes accessed | tf_op | source)
XLA Modules:
  0.0 146.4 jit_solution(10323588897234355310)
XLA Ops:
  0.0 4.0 %shard_map.73 = (bf16[16,64,128]{2,1,0:T(8,128)(2,1)}, f32[16,128]{1,0:T(8,128)}, bf16[168,1536]{1,0:T(8,128)(2,1)}, bf16[168,1536]{1,0:T(8,128)(2,1)}, bf16[168,1536]{1,0:T(8,128)(2,1)}) custom-call(s32[1,4]{1,0:T(1,128)} %lengths.1, s32[4,128]{1,0:T(4,128)} %bitcast.23, f32[4,128]{1,0:T(4,128)} %bitcast.24, bf16[192,128]{1,0:T(8,128)(2,1)} %bitcast.22, ...), custom_call_target="tpu_custom_call" | custom-call | tf_op jit(solution)/shard_map/pallas_call | solution.py:319
  4.1 15.2 %all-to-all-start = ((bf16[16,64,128]{2,1,0:T(8,128)(2,1)}), bf16[16,64,128]{2,1,0:T(8,128)(2,1)S(1)}, u32[]{:S(2)}, u32[]{:S(2)}) async-start(bf16[16,64,128]{2,1,0:T(8,128)(2,1)} %get-tuple-element.33), calls=%async_computation | async-start | bytes 524288 | tf_op jit(solution)/shard_map/all_to_all | solution.py:330
  19.3 4.2 %collective-permute-start = (bf16[168,1536]{1,0:T(8,128)(2,1)}, bf16[168,1536]{1,0:T(8,128)(2,1)S(1)}, u32[]{:S(2)}, u32[]{:S(2)}) collective-permute-start(bf16[168,1536]{1,0:T(8,128)(2,1)} %get-tuple-element.34), channel_id=1, source_target_pairs={{0,64},{16,80},{32,96},{48,112},{64,0},{80,16},{96,32},{112,48},{1... | collective-permute-start | bytes 1548296 | tf_op jit(solution)/shard_map/ppermute | solution.py:291
  23.5 1.9 %collective-permute-start.1 = (bf16[168,1536]{1,0:T(8,128)(2,1)}, bf16[168,1536]{1,0:T(8,128)(2,1)S(1)}, u32[]{:S(2)}, u32[]{:S(2)}) collective-permute-start(bf16[168,1536]{1,0:T(8,128)(2,1)} %get-tuple-element.35), channel_id=1, source_target_pairs={{0,32},{16,48},{32,64},{48,80},{64,96},{80,112},{96,0},{112,16},{1... | collective-permute-start | bytes 1548296 | tf_op jit(solution)/shard_map/ppermute | solution.py:291
  25.4 3.9 %collective-permute-start.2 = (bf16[168,1536]{1,0:T(8,128)(2,1)}, bf16[168,1536]{1,0:T(8,128)(2,1)S(1)}, u32[]{:S(2)}, u32[]{:S(2)}) collective-permute-start(bf16[168,1536]{1,0:T(8,128)(2,1)} %get-tuple-element.36), channel_id=1, source_target_pairs={{0,96},{16,112},{32,0},{48,16},{64,32},{80,48},{96,64},{112,80},{1... | collective-permute-start | bytes 1548296 | tf_op jit(solution)/shard_map/ppermute | solution.py:291
  29.3 7.9 %all-to-all-done.in_ref = bf16[16,64,128]{2,1,0:T(8,128)(2,1)S(1)} async-done(((bf16[16,64,128]{2,1,0:T(8,128)(2,1)}), bf16[16,64,128]{2,1,0:T(8,128)(2,1)S(1)}, u32[]{:S(2)}, u32[]{:S(2)}) %all-to-all-start) | async-done | bytes 262176 | tf_op jit(solution)/shard_map/all_to_all | solution.py:330
  37.2 0.3 shard_map.74
  37.5 14.8 %all-gather = bf16[768,640]{1,0:T(8,128)(2,1)S(1)} all-gather(bf16[192,640]{1,0:T(8,128)(2,1)S(1)} %shard_map.74), channel_id=2, replica_groups={{0,128,256,384},{16,144,272,400},{32,160,288,416},{48,176,304,432},{64,..., dimensions={0}, use_global_device_ids=true | all-gather | bytes 1228800 | tf_op jit(solution)/shard_map/all_gather | solution.py:47
  52.3 0.0 collective-permute-done.refs_2_
  52.3 0.0 collective-permute-done.1.refs_1_
  52.3 0.0 collective-permute-done.2.refs_3_
  52.3 1.9 %collective-permute-start.3 = (bf16[4,192,640]{2,1,0:T(8,128)(2,1)S(1)}, bf16[4,192,640]{2,1,0:T(8,128)(2,1)S(1)}, u32[]{:S(2)}, u32[]{:S(2)}) collective-permute-start(bf16[4,192,640]{2,1,0:T(8,128)(2,1)S(1)} %bitcast.14), channel_id=1, source_target_pairs={{0,16},{16,0},{32,48},{48,32},{64,80},{80,64},{96,112},{112,96},{1... | collective-permute-start | bytes 2949128 | tf_op jit(solution)/shard_map/ppermute | solution.py:352
  54.2 0.1 pad_add_fusion.place
  54.3 2.9 %shard_map.75 = (bf16[192,1344]{1,0:T(8,128)(2,1)}, bf16[192,1344]{1,0:T(8,128)(2,1)}, bf16[192,1344]{1,0:T(8,128)(2,1)}, bf16[192,1344]{1,0:T(8,128)(2,1)}, bf16[168,1536]{1,0:T(8,128)(2,1)}) custom-call(bf16[192,5376]{1,0:T(8,128)(2,1)} %bitcast.21, bf16[168,6144]{1,0:T(8,128)(2,1)} %bitcast.20), custom_call_target="tpu_custom_call" | custom-call | tf_op jit(solution)/shard_map/pallas_call | solution.py:337
  57.2 0.0 collective-permute-done.3.other_ref
  57.2 0.0 copy-start.1
  57.3 1.0 copy-done.1
  58.3 3.5 %shard_map.76 = bf16[4,168,640]{2,1,0:T(8,128)(2,1)} custom-call(s32[3]{0:T(128)S(1)} %pad_add_fusion.place, bf16[4,192,640]{2,1,0:T(8,128)(2,1)S(1)} %bitcast.15, bf16[4,192,640]{2,1,0:T(8,128)(2,1)S(1)} %collective-permute-done.3.other_ref, bf16[168,1536]{1,0:T(8,128)(2,1)S(1)} %copy-done.1, bf16[168,1536]{1,0:T(8,128)(2,1)S(1)} %collective-permute-done.1.refs_1_, ...), custom_call_target="tpu_custom_call" | custom-call | tf_op jit(solution)/shard_map/pallas_call | solution.py:296
  61.8 4.9 %all-to-all-start.1 = ((bf16[4,168,640]{2,1,0:T(8,128)(2,1)}), bf16[4,168,640]{2,1,0:T(8,128)(2,1)S(1)}, u32[]{:S(2)}, u32[]{:S(2)}) async-start(bf16[4,168,640]{2,1,0:T(8,128)(2,1)} %shard_map.76), calls=%async_computation.1 | async-start | bytes 1720320 | tf_op jit(solution)/shard_map/all_to_all | solution.py:43
  66.7 3.3 %collective-permute-start.4 = (bf16[192,1344]{1,0:T(8,128)(2,1)}, bf16[192,1344]{1,0:T(8,128)(2,1)S(1)}, u32[]{:S(2)}, u32[]{:S(2)}) collective-permute-start(bf16[192,1344]{1,0:T(8,128)(2,1)} %get-tuple-element.48), channel_id=1, source_target_pairs={{0,256},{16,272},{32,288},{48,304},{64,320},{80,336},{96,352},{112... | collective-permute-start | bytes 1548296 | tf_op jit(solution)/shard_map/ppermute | solution.py:291
  70.0 4.1 %collective-permute-start.5 = (bf16[192,1344]{1,0:T(8,128)(2,1)}, bf16[192,1344]{1,0:T(8,128)(2,1)S(1)}, u32[]{:S(2)}, u32[]{:S(2)}) collective-permute-start(bf16[192,1344]{1,0:T(8,128)(2,1)} %get-tuple-element.49), channel_id=1, source_target_pairs={{0,128},{16,144},{32,160},{48,176},{64,192},{80,208},{96,224},{112... | collective-permute-start | bytes 1548296 | tf_op jit(solution)/shard_map/ppermute | solution.py:291
  74.1 3.0 %collective-permute-start.6 = (bf16[192,1344]{1,0:T(8,128)(2,1)}, bf16[192,1344]{1,0:T(8,128)(2,1)S(1)}, u32[]{:S(2)}, u32[]{:S(2)}) collective-permute-start(bf16[192,1344]{1,0:T(8,128)(2,1)} %get-tuple-element.50), channel_id=1, source_target_pairs={{0,384},{16,400},{32,416},{48,432},{64,448},{80,464},{96,480},{112... | collective-permute-start | bytes 1548296 | tf_op jit(solution)/shard_map/ppermute | solution.py:291
  77.1 1.9 %all-to-all-done.1.in_ref = bf16[4,168,640]{2,1,0:T(8,128)(2,1)S(1)} async-done(((bf16[4,168,640]{2,1,0:T(8,128)(2,1)}), bf16[4,168,640]{2,1,0:T(8,128)(2,1)S(1)}, u32[]{:S(2)}, u32[]{:S(2)}) %all-to-all-start.1) | async-done | bytes 860192 | tf_op jit(solution)/shard_map/all_to_all | solution.py:43
  79.0 0.0 copy-start.2
  79.0 0.9 copy-done.2
  79.9 0.2 shard_map.77
  80.1 0.0 copy-start
  80.1 13.0 %all-gather.1 = bf16[672,640]{1,0:T(8,128)(2,1)S(1)} all-gather(bf16[168,640]{1,0:T(8,128)(2,1)S(1)} %shard_map.77), channel_id=3, replica_groups={{0,32,64,96},{16,48,80,112},{128,160,192,224},{144,176,208,240},{256,28..., dimensions={0}, use_global_device_ids=true | all-gather | bytes 1075200 | tf_op jit(solution)/shard_map/all_gather | solution.py:47
  93.1 0.0 collective-permute-done.4.refs_0_
  93.1 2.9 %collective-permute-done.5.refs_1_ = bf16[192,1344]{1,0:T(8,128)(2,1)S(1)} collective-permute-done((bf16[192,1344]{1,0:T(8,128)(2,1)}, bf16[192,1344]{1,0:T(8,128)(2,1)S(1)}, u32[]{:S(2)}, u32[]{:S(2)}) %collective-permute-start.5) | collective-permute-done | bytes 516128 | tf_op jit(solution)/shard_map/ppermute | solution.py:291
  96.0 0.1 collective-permute-done.6.refs_2_
  96.1 1.9 %collective-permute-start.7 = (bf16[4,168,640]{2,1,0:T(8,128)(2,1)S(1)}, bf16[4,168,640]{2,1,0:T(8,128)(2,1)S(1)}, u32[]{:S(2)}, u32[]{:S(2)}) collective-permute-start(bf16[4,168,640]{2,1,0:T(8,128)(2,1)S(1)} %bitcast.16), channel_id=1, source_target_pairs={{0,16},{16,0},{32,48},{48,32},{64,80},{80,64},{96,112},{112,96},{1... | collective-permute-start | bytes 2580488 | tf_op jit(solution)/shard_map/ppermute | solution.py:359
  98.0 2.4 %collective-permute-done.7.other_ref = bf16[4,168,640]{2,1,0:T(8,128)(2,1)S(1)} collective-permute-done((bf16[4,168,640]{2,1,0:T(8,128)(2,1)S(1)}, bf16[4,168,640]{2,1,0:T(8,128)(2,1)S(1)}, u32[]{:S(2)}, u32[]{:S(2)}) %collective-permute-start.7) | collective-permute-done | bytes 860192 | tf_op jit(solution)/shard_map/ppermute | solution.py:359
  100.4 2.2 %shard_map.78 = (bf16[1344,640]{1,0:T(8,128)(2,1)S(1)}, bf16[192,640]{1,0:T(8,128)(2,1)S(1)}, bf16[192,640]{1,0:T(8,128)(2,1)S(1)}, bf16[192,640]{1,0:T(8,128)(2,1)S(1)}) custom-call(s32[3]{0:T(128)S(1)} %pad_add_fusion.place, bf16[4,168,640]{2,1,0:T(8,128)(2,1)S(1)} %bitcast.17, bf16[4,168,640]{2,1,0:T(8,128)(2,1)S(1)} %collective-permute-done.7.other_ref, ...), custom_call_target="tpu_custom_call" | custom-call | flops 330301440 | bytes 2236416 | tf_op jit(solution)/shard_map/pallas_call | solution.py:362
  102.6 4.0 %collective-permute-start.8 = (bf16[192,640]{1,0:T(8,128)(2,1)S(1)}, bf16[192,640]{1,0:T(8,128)(2,1)S(1)}, u32[]{:S(2)}, u32[]{:S(2)}) collective-permute-start(bf16[192,640]{1,0:T(8,128)(2,1)S(1)} %get-tuple-element.55), channel_id=1, source_target_pairs={{0,256},{16,272},{32,288},{48,304},{64,320},{80,336},{96,352},{112... | collective-permute-start | bytes 737288 | tf_op jit(solution)/shard_map/ppermute | solution.py:291
  106.6 3.9 %collective-permute-start.9 = (bf16[192,640]{1,0:T(8,128)(2,1)S(1)}, bf16[192,640]{1,0:T(8,128)(2,1)S(1)}, u32[]{:S(2)}, u32[]{:S(2)}) collective-permute-start(bf16[192,640]{1,0:T(8,128)(2,1)S(1)} %get-tuple-element.56), channel_id=1, source_target_pairs={{0,384},{16,400},{32,416},{48,432},{64,448},{80,464},{96,480},{112... | collective-permute-start | bytes 737288 | tf_op jit(solution)/shard_map/ppermute | solution.py:291
  110.5 1.9 %collective-permute-start.10 = (bf16[192,640]{1,0:T(8,128)(2,1)S(1)}, bf16[192,640]{1,0:T(8,128)(2,1)S(1)}, u32[]{:S(2)}, u32[]{:S(2)}) collective-permute-start(bf16[192,640]{1,0:T(8,128)(2,1)S(1)} %get-tuple-element.57), channel_id=1, source_target_pairs={{0,128},{16,144},{32,160},{48,176},{64,192},{80,208},{96,224},{112... | collective-permute-start | bytes 737288 | tf_op jit(solution)/shard_map/ppermute | solution.py:291
  112.5 0.0 copy-done
  112.5 0.0 copy-start.3
  112.5 0.6 shard_map.79.refs_3_
  113.1 0.9 collective-permute-done.8.refs_0_
  114.0 5.2 %collective-permute-done.9.refs_1_ = bf16[192,640]{1,0:T(8,128)(2,1)S(1)} collective-permute-done((bf16[192,640]{1,0:T(8,128)(2,1)S(1)}, bf16[192,640]{1,0:T(8,128)(2,1)S(1)}, u32[]{:S(2)}, u32[]{:S(2)}) %collective-permute-start.9) | collective-permute-done | bytes 245792 | tf_op jit(solution)/shard_map/ppermute | solution.py:291
  119.2 1.9 %collective-permute-done.10.refs_2_ = bf16[192,640]{1,0:T(8,128)(2,1)S(1)} collective-permute-done((bf16[192,640]{1,0:T(8,128)(2,1)S(1)}, bf16[192,640]{1,0:T(8,128)(2,1)S(1)}, u32[]{:S(2)}, u32[]{:S(2)}) %collective-permute-start.10) | collective-permute-done | bytes 245792 | tf_op jit(solution)/shard_map/ppermute | solution.py:291
  121.1 0.3 shard_map.80
  121.4 23.8 %all_to_all.15.in_ref = bf16[16,64,128]{2,1,0:T(8,128)(2,1)S(1)} all-to-all(bf16[16,64,128]{2,1,0:T(8,128)(2,1)S(1)} %shard_map.80), channel_id=1, replica_groups=mesh['dp'=32,'expert'=16] {'expert'}, dimensions={0} | all-to-all | bytes 524288 | tf_op jit(solution)/shard_map/all_to_all | solution.py:368
  145.2 0.0 copy-done.3
  145.2 1.1 shard_map.81
Async XLA Ops:
  4.1 33.1 %all-to-all-start = ((bf16[16,64,128]{2,1,0:T(8,128)(2,1)}), bf16[16,64,128]{2,1,0:T(8,128)(2,1)S(1)}, u32[]{:S(2)}, u32[]{:S(2)}) async-start(bf16[16,64,128]{2,1,0:T(8,128)(2,1)} %get-tuple-element.33), calls=%async_computation | async-start | bytes 524288 | tf_op jit(solution)/shard_map/all_to_all | solution.py:330
  19.3 33.0 %collective-permute-start = (bf16[168,1536]{1,0:T(8,128)(2,1)}, bf16[168,1536]{1,0:T(8,128)(2,1)S(1)}, u32[]{:S(2)}, u32[]{:S(2)}) collective-permute-start(bf16[168,1536]{1,0:T(8,128)(2,1)} %get-tuple-element.34), channel_id=1, source_target_pairs={{0,64},{16,80},{32,96},{48,112},{64,0},{80,16},{96,32},{112,48},{1... | collective-permute-start | bytes 1548296 | tf_op jit(solution)/shard_map/ppermute | solution.py:291
  23.5 28.8 %collective-permute-start.1 = (bf16[168,1536]{1,0:T(8,128)(2,1)}, bf16[168,1536]{1,0:T(8,128)(2,1)S(1)}, u32[]{:S(2)}, u32[]{:S(2)}) collective-permute-start(bf16[168,1536]{1,0:T(8,128)(2,1)} %get-tuple-element.35), channel_id=1, source_target_pairs={{0,32},{16,48},{32,64},{48,80},{64,96},{80,112},{96,0},{112,16},{1... | collective-permute-start | bytes 1548296 | tf_op jit(solution)/shard_map/ppermute | solution.py:291
  25.4 26.9 %collective-permute-start.2 = (bf16[168,1536]{1,0:T(8,128)(2,1)}, bf16[168,1536]{1,0:T(8,128)(2,1)S(1)}, u32[]{:S(2)}, u32[]{:S(2)}) collective-permute-start(bf16[168,1536]{1,0:T(8,128)(2,1)} %get-tuple-element.36), channel_id=1, source_target_pairs={{0,96},{16,112},{32,0},{48,16},{64,32},{80,48},{96,64},{112,80},{1... | collective-permute-start | bytes 1548296 | tf_op jit(solution)/shard_map/ppermute | solution.py:291
  52.3 4.9 %collective-permute-start.3 = (bf16[4,192,640]{2,1,0:T(8,128)(2,1)S(1)}, bf16[4,192,640]{2,1,0:T(8,128)(2,1)S(1)}, u32[]{:S(2)}, u32[]{:S(2)}) collective-permute-start(bf16[4,192,640]{2,1,0:T(8,128)(2,1)S(1)} %bitcast.14), channel_id=1, source_target_pairs={{0,16},{16,0},{32,48},{48,32},{64,80},{80,64},{96,112},{112,96},{1... | collective-permute-start | bytes 2949128 | tf_op jit(solution)/shard_map/ppermute | solution.py:352
  57.2 1.0 copy-start.1
  61.8 17.2 %all-to-all-start.1 = ((bf16[4,168,640]{2,1,0:T(8,128)(2,1)}), bf16[4,168,640]{2,1,0:T(8,128)(2,1)S(1)}, u32[]{:S(2)}, u32[]{:S(2)}) async-start(bf16[4,168,640]{2,1,0:T(8,128)(2,1)} %shard_map.76), calls=%async_computation.1 | async-start | bytes 1720320 | tf_op jit(solution)/shard_map/all_to_all | solution.py:43
  66.7 26.4 %collective-permute-start.4 = (bf16[192,1344]{1,0:T(8,128)(2,1)}, bf16[192,1344]{1,0:T(8,128)(2,1)S(1)}, u32[]{:S(2)}, u32[]{:S(2)}) collective-permute-start(bf16[192,1344]{1,0:T(8,128)(2,1)} %get-tuple-element.48), channel_id=1, source_target_pairs={{0,256},{16,272},{32,288},{48,304},{64,320},{80,336},{96,352},{112... | collective-permute-start | bytes 1548296 | tf_op jit(solution)/shard_map/ppermute | solution.py:291
  70.0 25.9 %collective-permute-start.5 = (bf16[192,1344]{1,0:T(8,128)(2,1)}, bf16[192,1344]{1,0:T(8,128)(2,1)S(1)}, u32[]{:S(2)}, u32[]{:S(2)}) collective-permute-start(bf16[192,1344]{1,0:T(8,128)(2,1)} %get-tuple-element.49), channel_id=1, source_target_pairs={{0,128},{16,144},{32,160},{48,176},{64,192},{80,208},{96,224},{112... | collective-permute-start | bytes 1548296 | tf_op jit(solution)/shard_map/ppermute | solution.py:291
  74.1 22.0 %collective-permute-start.6 = (bf16[192,1344]{1,0:T(8,128)(2,1)}, bf16[192,1344]{1,0:T(8,128)(2,1)S(1)}, u32[]{:S(2)}, u32[]{:S(2)}) collective-permute-start(bf16[192,1344]{1,0:T(8,128)(2,1)} %get-tuple-element.50), channel_id=1, source_target_pairs={{0,384},{16,400},{32,416},{48,432},{64,448},{80,464},{96,480},{112... | collective-permute-start | bytes 1548296 | tf_op jit(solution)/shard_map/ppermute | solution.py:291
  79.0 0.9 copy-start.2
  80.1 32.4 %copy-start = (bf16[192,1344]{1,0:T(8,128)(2,1)S(1)}, bf16[192,1344]{1,0:T(8,128)(2,1)}, u32[]{:S(2)}) copy-start(bf16[192,1344]{1,0:T(8,128)(2,1)} %get-tuple-element.58.weights) | copy-start | bytes 1548292
  96.1 4.3 %collective-permute-start.7 = (bf16[4,168,640]{2,1,0:T(8,128)(2,1)S(1)}, bf16[4,168,640]{2,1,0:T(8,128)(2,1)S(1)}, u32[]{:S(2)}, u32[]{:S(2)}) collective-permute-start(bf16[4,168,640]{2,1,0:T(8,128)(2,1)S(1)} %bitcast.16), channel_id=1, source_target_pairs={{0,16},{16,0},{32,48},{48,32},{64,80},{80,64},{96,112},{112,96},{1... | collective-permute-start | bytes 2580488 | tf_op jit(solution)/shard_map/ppermute | solution.py:359
  102.6 11.4 %collective-permute-start.8 = (bf16[192,640]{1,0:T(8,128)(2,1)S(1)}, bf16[192,640]{1,0:T(8,128)(2,1)S(1)}, u32[]{:S(2)}, u32[]{:S(2)}) collective-permute-start(bf16[192,640]{1,0:T(8,128)(2,1)S(1)} %get-tuple-element.55), channel_id=1, source_target_pairs={{0,256},{16,272},{32,288},{48,304},{64,320},{80,336},{96,352},{112... | collective-permute-start | bytes 737288 | tf_op jit(solution)/shard_map/ppermute | solution.py:291
  106.6 12.6 %collective-permute-start.9 = (bf16[192,640]{1,0:T(8,128)(2,1)S(1)}, bf16[192,640]{1,0:T(8,128)(2,1)S(1)}, u32[]{:S(2)}, u32[]{:S(2)}) collective-permute-start(bf16[192,640]{1,0:T(8,128)(2,1)S(1)} %get-tuple-element.56), channel_id=1, source_target_pairs={{0,384},{16,400},{32,416},{48,432},{64,448},{80,464},{96,480},{112... | collective-permute-start | bytes 737288 | tf_op jit(solution)/shard_map/ppermute | solution.py:291
  110.5 10.5 %collective-permute-start.10 = (bf16[192,640]{1,0:T(8,128)(2,1)S(1)}, bf16[192,640]{1,0:T(8,128)(2,1)S(1)}, u32[]{:S(2)}, u32[]{:S(2)}) collective-permute-start(bf16[192,640]{1,0:T(8,128)(2,1)S(1)} %get-tuple-element.57), channel_id=1, source_target_pairs={{0,128},{16,144},{32,160},{48,176},{64,192},{80,208},{96,224},{112... | collective-permute-start | bytes 737288 | tf_op jit(solution)/shard_map/ppermute | solution.py:291
  112.5 32.8 %copy-start.3 = (f32[16,128]{1,0:T(8,128)S(1)}, f32[16,128]{1,0:T(8,128)}, u32[]{:S(2)}) copy-start(f32[16,128]{1,0:T(8,128)} %get-tuple-element.60.slot_ref) | copy-start | bytes 24580
